TPU v7x, 512 devices: a whole 4x4x16 slice. The times are simulated.
512 devices in a mesh: wide: 32 (over z_lo, x), narrow: 16 (over y, z_hi, core).
Axes of the slice: x: 4, y: 4, z: 16 (z_hi: 2, z_lo: 8; z = z_hi * 8 + z_lo), core: 2. Of those that a mesh axis runs over, the one named last changes fastest.
Arguments:
- a_blocks: bfloat16 [8192, 7, 4096], P(('wide', 'narrow')), may hold values from -0.25 to 0.25
- p_blocks: bfloat16 [8192, 4096], P(('wide', 'narrow')), may hold values from -0.75 to 0.75
- columns: int32 [8192, 7], P(('wide', 'narrow')), may hold values from 0 to 8191, as said below
- aggregate: int32 [8192], P(('wide', 'narrow')), may hold values from 0 to 511, as said below
- target: int32 [8192, 7], P(('wide', 'narrow')), may hold values from 0 to 6
Outputs:
- coarse: float32 [512, 7, 4096], P(('wide', 'narrow'))
Inputs may be any that keep to these rules, and one draw needn't show every extreme that they name: columns[i,0] = i; every entry lies within 16 of its row i, and entries i + 16 or i - 16 occur in every row. Fine block row i belongs to an aggregate of its own pair of planes: aggregate[i] // 2 = i // 32; every aggregate has a fine block row.
All inputs are finite; a program needn't handle non-finite values.
Results may differ from a plain program's by a relative error of at most 0.0029.
Values may be sent and summed in bfloat16 or wider, within the bound.
A program may use at most 64 MiB of HBM per device.

v0:
```python
import jax
import jax.numpy as jnp
from jax import lax
from jax.sharding import PartitionSpec as P

B = 64
K = 7
KC = 7
CR_DEV = 1


def padded(block, sides, width):
    for axis, dim in sides:
        count = lax.axis_size(axis)
        forward = [(i, i + 1) for i in range(count - 1)]
        backward = [(target, source) for source, target in forward]
        low = lax.ppermute(
            lax.slice_in_dim(block, block.shape[dim] - width, None, axis=dim), axis, forward
        )
        high = lax.ppermute(lax.slice_in_dim(block, 0, width, axis=dim), axis, backward)
        block = jnp.concatenate([low, block, high], axis=dim)
    return block


def from_partner(shard, axis, stride):
    return lax.ppermute(shard, axis, [(i, i ^ 1 << stride) for i in range(lax.axis_size(axis))])


def local(a_blocks, p_blocks, columns, aggregate, target):
    block_rows = a_blocks.shape[0]
    wide_index = lax.axis_index("wide")
    narrow_count = lax.axis_size("narrow")
    narrow_index = lax.axis_index("narrow")
    device_index = wide_index * narrow_count + narrow_index
    extended = padded(p_blocks, ((("wide", "narrow"), 0),), block_rows)
    root = device_index * block_rows - block_rows
    local_cols = columns - root
    picked = jnp.take(extended, local_cols, axis=0).reshape(block_rows, K, B, B)
    a_matrix = a_blocks.reshape(block_rows, K, B, B)
    applied = jnp.einsum(
        "rkcd,rkde->rkce", a_matrix, picked, preferred_element_type=jnp.float32
    ).astype(jnp.bfloat16)
    owned = p_blocks.reshape(block_rows, B, B)
    pair_count = 2 * CR_DEV
    pair_start = device_index // 2 * pair_count
    parity = narrow_index % 2
    other_applied, other_p, other_agg, other_target = from_partner(
        (applied, p_blocks, aggregate, target), "narrow", 0
    )
    other_products = jnp.einsum(
        "rca,rkcb->rkab",
        other_p.reshape(block_rows, B, B),
        other_applied,
        preferred_element_type=jnp.float32,
    )
    own_products = jnp.einsum("rca,rkcb->rkab", owned, applied, preferred_element_type=jnp.float32)
    all_products = jnp.concatenate(
        [
            own_products.reshape(block_rows * K, B * B),
            other_products.reshape(block_rows * K, B * B),
        ],
        axis=0,
    )
    own_start = pair_start + parity * CR_DEV
    all_agg = jnp.concatenate([aggregate, other_agg], axis=0)
    all_target = jnp.concatenate([target, other_target], axis=0)
    keys_here = ((all_agg - own_start)[:, None] * KC + all_target).reshape(-1)
    wanted = jnp.arange(CR_DEV * KC, dtype=jnp.int32)
    selector = (wanted[:, None] == keys_here[None, :]).astype(jnp.float32)
    own_terms = jnp.dot(
        selector, all_products, precision=lax.Precision.HIGHEST, preferred_element_type=jnp.float32
    )
    return own_terms.reshape(CR_DEV, KC, B * B)


def solution(mesh):
    placed = (
        P(("wide", "narrow"), None, None),
        P(("wide", "narrow"), None),
        P(("wide", "narrow"), None),
        P(("wide", "narrow")),
        P(("wide", "narrow"), None),
    )
    return jax.shard_map(
        local,
        mesh=mesh,
        in_specs=placed,
        out_specs=P(("wide", "narrow"), None, None),
        check_vma=False,
    )
```

profile of v0, /device:TPU:31, one launch (start us, length us, event | category | flops | bytes accessed | tf_op | source)
XLA Modules:
  0.0 84.2 jit_solution(353380830053491757)
XLA Ops:
  0.0 0.0 copy-start
  0.0 16.1 %collective-permute-start.2 = (bf16[16,4096]{1,0:T(8,128)(2,1)}, bf16[16,4096]{1,0:T(8,128)(2,1)S(1)}, u32[]{:S(2)}, u32[]{:S(2)}) collective-permute-start(bf16[16,4096]{1,0:T(8,128)(2,1)} %param.6), channel_id=1, source_target_pairs={{0,1},{1,2},{2,3},{3,4},{4,5},{5,6},{6,7},{7,8},{8,9},{9,10},{10,1... | collective-permute-start | bytes 393224 | tf_op jit(solution)/shard_map/ppermute | solution.py:17
  16.1 1.9 %collective-permute-start.3 = (bf16[16,4096]{1,0:T(8,128)(2,1)}, bf16[16,4096]{1,0:T(8,128)(2,1)S(1)}, u32[]{:S(2)}, u32[]{:S(2)}) collective-permute-start(bf16[16,4096]{1,0:T(8,128)(2,1)} %param.6), channel_id=1, source_target_pairs={{1,0},{2,1},{3,2},{4,3},{5,4},{6,5},{7,6},{8,7},{9,8},{10,9},{11,1... | collective-permute-start | bytes 393224 | tf_op jit(solution)/shard_map/ppermute | solution.py:20
  18.1 0.7 compare_and_fusion
  18.8 0.1 copy.13
  18.8 0.1 reshape.62
  18.9 0.1 copy.12
  19.0 3.8 %reshape.54 = bf16[16,7,64,64]{3,2,0,1:T(8,128)(2,1)} reshape(bf16[16,7,4096]{2,0,1:T(8,128)(2,1)} %param.5) | data formatting | bytes 1835008 | tf_op jit(solution)/shard_map/reshape | solution.py:39
  22.8 0.0 collective-permute-done.2
  22.8 12.3 %collective-permute-done.3 = bf16[16,4096]{1,0:T(8,128)(2,1)S(1)} collective-permute-done((bf16[16,4096]{1,0:T(8,128)(2,1)}, bf16[16,4096]{1,0:T(8,128)(2,1)S(1)}, u32[]{:S(2)}, u32[]{:S(2)}) %collective-permute-start.3) | collective-permute-done | bytes 131104 | tf_op jit(solution)/shard_map/ppermute | solution.py:20
  35.2 0.0 copy-done
  35.2 1.1 %gather_fusion = bf16[112,4096]{1,0:T(8,128)(2,1)S(1)} fusion(bf16[48,4096]{1,0:T(8,128)(2,1)S(1)} %pad_maximum_fusion, s32[1024]{0:T(1024)S(1)} %pad_clamp_fusion), kind=kCustom, calls=%fused_computation | custom fusion | bytes 1835456 | tf_op jit(solution)/shard_map/jit(_take)/gather | solution.py:38
  36.3 2.0 %gather.7 = bf16[16,7,64,64]{3,2,1,0:T(8,128)(2,1)S(1)} reshape(bf16[112,4096]{1,0:T(8,128)(2,1)S(1)} %gather_fusion) | data formatting | bytes 1835008 | tf_op jit(solution)/shard_map/jit(_take)/gather | solution.py:38
  38.3 2.6 %copy.14 = bf16[16,7,64,64]{2,3,1,0:T(8,128)(2,1)} copy(bf16[16,7,64,64]{3,2,1,0:T(8,128)(2,1)S(1)} %gather.7) | data formatting | bytes 1835008 | tf_op jit(solution)/shard_map/jit(_take)/gather | solution.py:38
  41.0 0.0 copy-start.2
  41.0 0.0 copy-start.1
  41.0 4.5 %convert_bitcast_fusion = bf16[16,7,64,64]{2,3,1,0:T(8,128)(2,1)} fusion(bf16[16,7,64,64]{3,2,0,1:T(8,128)(2,1)} %reshape.54, bf16[16,7,64,64]{2,3,1,0:T(8,128)(2,1)} %copy.14, pred[16,7]{1,0:T(8,128)(4,1)S(1)} %copy.12), kind=kOutput, calls=%fused_computation.9 | convolution fusion | flops 59637760 | bytes 2752624 | tf_op jit(solution)/shard_map/rkcd,rkde->rkce/dot_general | solution.py:40
  45.5 1.9 %collective-permute-start.4 = (bf16[16,7,64,64]{2,3,1,0:T(8,128)(2,1)}, bf16[16,7,64,64]{2,3,1,0:T(8,128)(2,1)}, u32[]{:S(2)}, u32[]{:S(2)}) collective-permute-start(bf16[16,7,64,64]{2,3,1,0:T(8,128)(2,1)} %convert_bitcast_fusion), channel_id=1, source_target_pairs={{0,1},{1,0},{2,3},{3,2},{4,5},{5,4},{6,7},{7,6},{8,9},{9,8},{10,11... | collective-permute-start | bytes 2752520 | tf_op jit(solution)/shard_map/ppermute | solution.py:26
  47.4 2.4 %collective-permute-start.5 = (bf16[16,4096]{1,0:T(8,128)(2,1)S(1)}, bf16[16,4096]{1,0:T(8,128)(2,1)S(1)}, u32[]{:S(2)}, u32[]{:S(2)}) collective-permute-start(bf16[16,4096]{1,0:T(8,128)(2,1)S(1)} %copy-done), channel_id=1, source_target_pairs={{0,1},{1,0},{2,3},{3,2},{4,5},{5,4},{6,7},{7,6},{8,9},{9,8},{10,11... | collective-permute-start | bytes 393224 | tf_op jit(solution)/shard_map/ppermute | solution.py:26
  49.8 0.0 copy-done.2
  49.8 1.9 %collective-permute-start = (s32[16]{0:T(128)S(1)}, s32[16]{0:T(128)S(1)}, u32[]{:S(2)}, u32[]{:S(2)}) collective-permute-start(s32[16]{0:T(128)S(1)} %copy-done.2), channel_id=1, source_target_pairs={{0,1},{1,0},{2,3},{3,2},{4,5},{5,4},{6,7},{7,6},{8,9},{9,8},{10,11... | collective-permute-start | bytes 200 | tf_op jit(solution)/shard_map/ppermute | solution.py:26
  51.7 0.0 copy-done.1
  51.8 2.4 %collective-permute-start.1 = (s32[16,7]{0,1:T(8,128)S(1)}, s32[16,7]{0,1:T(8,128)S(1)}, u32[]{:S(2)}, u32[]{:S(2)}) collective-permute-start(s32[16,7]{0,1:T(8,128)S(1)} %copy-done.1), channel_id=1, source_target_pairs={{0,1},{1,0},{2,3},{3,2},{4,5},{5,4},{6,7},{7,6},{8,9},{9,8},{10,11... | collective-permute-start | bytes 1352 | tf_op jit(solution)/shard_map/ppermute | solution.py:26
  54.2 0.2 reshape.71
  54.5 0.0 collective-permute-done
  54.5 0.1 fusion.15
  54.5 0.4 collective-permute-done.1
  55.0 0.1 add_add_fusion
  55.0 0.1 copy.11
  55.1 0.1 add.40
  55.2 3.9 %convolution_bitcast_fusion.2 = f32[16,7,64,64]{2,3,1,0:T(8,128)} fusion(bf16[16,7,64,64]{2,3,1,0:T(8,128)(2,1)} %convert_bitcast_fusion, bf16[16,64,64,1]{2,1,0,3:T(8,128)(2,1)S(1)} %reshape.71), kind=kOutput, calls=%fused_computation.6 | convolution fusion | flops 58720256 | bytes 2883584 | tf_op jit(solution)/shard_map/rca,rkcb->rkab/dot_general | solution.py:56
  59.2 5.0 %copy.16 = f32[16,7,64,64]{3,2,1,0:T(8,128)} copy(f32[16,7,64,64]{2,3,1,0:T(8,128)} %convolution_bitcast_fusion.2) | data formatting | bytes 3670016 | tf_op jit(solution)/shard_map/rca,rkcb->rkab/transpose | solution.py:56
  64.1 3.2 %reshape.56 = f32[112,4096]{1,0:T(8,128)S(1)} reshape(f32[16,7,64,64]{3,2,1,0:T(8,128)} %copy.16) | data formatting | bytes 3670016 | tf_op jit(solution)/shard_map/reshape | solution.py:59
  67.3 0.0 collective-permute-done.5
  67.3 0.2 reshape.72
  67.6 0.0 collective-permute-done.4
  67.6 3.9 %convolution_bitcast_fusion.1 = f32[16,7,64,64]{2,3,1,0:T(8,128)} fusion(bf16[16,7,64,64]{2,3,1,0:T(8,128)(2,1)} %collective-permute-done.4, bf16[16,64,64,1]{2,1,0,3:T(8,128)(2,1)S(1)} %reshape.72), kind=kOutput, calls=%fused_computation.5 | convolution fusion | flops 58720256 | bytes 2883584 | tf_op jit(solution)/shard_map/rca,rkcb->rkab/dot_general | solution.py:50
  71.5 5.0 %copy.17 = f32[16,7,64,64]{3,2,1,0:T(8,128)} copy(f32[16,7,64,64]{2,3,1,0:T(8,128)} %convolution_bitcast_fusion.1) | data formatting | bytes 3670016 | tf_op jit(solution)/shard_map/rca,rkcb->rkab/transpose | solution.py:50
  76.5 4.1 %reshape.58 = f32[112,4096]{1,0:T(8,128)} reshape(f32[16,7,64,64]{3,2,1,0:T(8,128)} %copy.17) | data formatting | bytes 3670016 | tf_op jit(solution)/shard_map/reshape | solution.py:60
  80.6 2.8 %convolution_bitcast_fusion = f32[1,7,4096]{2,1,0:T(8,128)S(1)} fusion(f32[112,4096]{1,0:T(8,128)} %reshape.58, f32[112,4096]{1,0:T(8,128)S(1)} %reshape.56, s32[224]{0:T(256)S(1)} %add.40), kind=kOutput, calls=%fused_computation.1 | convolution fusion | flops 77989408 | bytes 3785600 | tf_op jit(solution)/shard_map/dot_general | solution.py:70
  83.4 0.8 copy.18
  (2 shorter events, 0.0 us)
Async XLA Ops:
  0.0 35.2 %copy-start = (bf16[16,4096]{1,0:T(8,128)(2,1)S(1)}, bf16[16,4096]{1,0:T(8,128)(2,1)}, u32[]{:S(2)}) copy-start(bf16[16,4096]{1,0:T(8,128)(2,1)} %param.6) | copy-start | bytes 393220
  0.0 22.8 %collective-permute-start.2 = (bf16[16,4096]{1,0:T(8,128)(2,1)}, bf16[16,4096]{1,0:T(8,128)(2,1)S(1)}, u32[]{:S(2)}, u32[]{:S(2)}) collective-permute-start(bf16[16,4096]{1,0:T(8,128)(2,1)} %param.6), channel_id=1, source_target_pairs={{0,1},{1,2},{2,3},{3,4},{4,5},{5,6},{6,7},{7,8},{8,9},{9,10},{10,1... | collective-permute-start | bytes 393224 | tf_op jit(solution)/shard_map/ppermute | solution.py:17
  16.1 19.0 %collective-permute-start.3 = (bf16[16,4096]{1,0:T(8,128)(2,1)}, bf16[16,4096]{1,0:T(8,128)(2,1)S(1)}, u32[]{:S(2)}, u32[]{:S(2)}) collective-permute-start(bf16[16,4096]{1,0:T(8,128)(2,1)} %param.6), channel_id=1, source_target_pairs={{1,0},{2,1},{3,2},{4,3},{5,4},{6,5},{7,6},{8,7},{9,8},{10,9},{11,1... | collective-permute-start | bytes 393224 | tf_op jit(solution)/shard_map/ppermute | solution.py:20
  41.0 8.8 %copy-start.2 = (s32[16]{0:T(128)S(1)}, s32[16]{0:T(128)}, u32[]{:S(2)}) copy-start(s32[16]{0:T(128)} %param.8) | copy-start | bytes 196
  41.0 10.8 %copy-start.1 = (s32[16,7]{0,1:T(8,128)S(1)}, s32[16,7]{0,1:T(8,128)}, u32[]{:S(2)}) copy-start(s32[16,7]{0,1:T(8,128)} %param.9) | copy-start | bytes 1348
  45.5 22.1 %collective-permute-start.4 = (bf16[16,7,64,64]{2,3,1,0:T(8,128)(2,1)}, bf16[16,7,64,64]{2,3,1,0:T(8,128)(2,1)}, u32[]{:S(2)}, u32[]{:S(2)}) collective-permute-start(bf16[16,7,64,64]{2,3,1,0:T(8,128)(2,1)} %convert_bitcast_fusion), channel_id=1, source_target_pairs={{0,1},{1,0},{2,3},{3,2},{4,5},{5,4},{6,7},{7,6},{8,9},{9,8},{10,11... | collective-permute-start | bytes 2752520 | tf_op jit(solution)/shard_map/ppermute | solution.py:26
  47.4 19.9 %collective-permute-start.5 = (bf16[16,4096]{1,0:T(8,128)(2,1)S(1)}, bf16[16,4096]{1,0:T(8,128)(2,1)S(1)}, u32[]{:S(2)}, u32[]{:S(2)}) collective-permute-start(bf16[16,4096]{1,0:T(8,128)(2,1)S(1)} %copy-done), channel_id=1, source_target_pairs={{0,1},{1,0},{2,3},{3,2},{4,5},{5,4},{6,7},{7,6},{8,9},{9,8},{10,11... | collective-permute-start | bytes 393224 | tf_op jit(solution)/shard_map/ppermute | solution.py:26
  49.8 4.6 %collective-permute-start = (s32[16]{0:T(128)S(1)}, s32[16]{0:T(128)S(1)}, u32[]{:S(2)}, u32[]{:S(2)}) collective-permute-start(s32[16]{0:T(128)S(1)} %copy-done.2), channel_id=1, source_target_pairs={{0,1},{1,0},{2,3},{3,2},{4,5},{5,4},{6,7},{7,6},{8,9},{9,8},{10,11... | collective-permute-start | bytes 200 | tf_op jit(solution)/shard_map/ppermute | solution.py:26
  51.8 3.2 %collective-permute-start.1 = (s32[16,7]{0,1:T(8,128)S(1)}, s32[16,7]{0,1:T(8,128)S(1)}, u32[]{:S(2)}, u32[]{:S(2)}) collective-permute-start(s32[16,7]{0,1:T(8,128)S(1)} %copy-done.1), channel_id=1, source_target_pairs={{0,1},{1,0},{2,3},{3,2},{4,5},{5,4},{6,7},{7,6},{8,9},{9,8},{10,11... | collective-permute-start | bytes 1352 | tf_op jit(solution)/shard_map/ppermute | solution.py:26
where the time goes:
time: 84.8 us; the launch traced here: 84.2 us
  local copies, waits for them, and re-layouts  28.5 us (34%)
  starting transfers between devices  26.7 us (31%)
  matrix products  15.1 us (18%)
  waiting for transfers between devices  12.8 us (15%)
  other arithmetic  0.88 us (1%)
    ppermute x1, starting transfers between devices, padded(): lax.ppermute(lax.slice_in_dim(block, block.shape[dim] - width, None, axis...  16.1 us
    ppermute x1, waiting for transfers between devices, padded(): lax.ppermute(lax.slice_in_dim(block, 0, width, axis=dim), axis, backward)  12.3 us
    ppermute x4, starting transfers between devices, from_partner(): lax.ppermute(shard, axis, [(i, i ^ 1 << stride) for i in range(lax.axis_s...  8.64 us
    gather x3, local copies, waits for them, and re-layouts, local(): picked = jnp.take(extended, local_cols, axis=0).reshape(block_rows, K, B, B)  5.75 us
    transpose x1, local copies, waits for them, and re-layouts, local(): jnp.einsum('rca,rkcb->rkab', owned, applied, preferred_element_type=jnp.f...  4.98 us
    transpose x1, local copies, waits for them, and re-layouts, local(): jnp.einsum('rca,rkcb->rkab', other_p.reshape(block_rows, B, B), other_app...  4.98 us
    dot_general x1, matrix products, local(): jnp.einsum('rkcd,rkde->rkce', a_matrix, picked, preferred_element_type=jn...  4.51 us
    reshape x1, local copies, waits for them, and re-layouts, local(): other_products.reshape(block_rows * K, B * B)  4.13 us
  transfers between devices with their start and end apart: 6, of which 2 were waited for; matrix products, arithmetic and copies ran while one was open for 21% of the time, Pallas kernels for 0%

commit v1 on v0

v1 whole, which is shorter than its diff:
```python
import functools

import jax
import jax.numpy as jnp
from jax import lax
from jax.experimental import pallas as pl
from jax.experimental.pallas import tpu as pltpu
from jax.sharding import PartitionSpec as P

B = 64
K = 7
KC = 7
ROWS = 16
TILES = 32
LANES = 128
PAIRS = ((1, 2), (3, 4), (5, 6), (0, None))
GROUP = 4
X_CHIPS = 4
CHUNKS = 4
F32 = jnp.float32
BF16 = jnp.bfloat16
MESH = pl.DeviceIdType.MESH


def swap(x):
    return pltpu.roll(x, B, 1)


def kernel(
    n_wide,
    n_narrow,
    cols_hbm,
    agg_hbm,
    targ_hbm,
    p_hbm,
    a_hbm,
    out,
    cols,
    agg,
    targ,
    p_raw,
    a_raw,
    p_f32,
    a_f32,
    pair_f32,
    own_pairs,
    sib_pairs,
    passing,
    far_pairs,
    near_left,
    near_right,
    far_left,
    far_right,
    blocks,
    y_all,
    pm_f32,
    pm_t,
    acc,
    part_out,
    part_in,
    load_sem,
    send_sem,
    recv_sem,
):
    total = n_wide * n_narrow
    me = lax.axis_index("wide") * n_narrow + lax.axis_index("narrow")
    core = me % 2

    def place(index):
        return (index // n_narrow, index % n_narrow)

    def far_of(index):
        return (index - 1 + 2 * (index % 2) + total) % total

    def relay_of(index, flipped):
        wide, narrow = index // n_narrow, index % n_narrow
        z_lo, x = wide // X_CHIPS, wide % X_CHIPS
        flip = (z_lo + index % 2 + flipped) % 2
        z_hi = narrow // 2 % 2
        wide = (z_lo + 1 - 2 * (z_lo % 2)) * X_CHIPS + x
        return wide * n_narrow + narrow + flip * (2 - 4 * z_hi)

    partner = far_of(me)
    source = relay_of(me, 1)
    quick = (me // n_narrow // X_CHIPS + core) % 2 == 1
    sibling = place(me + 1 - 2 * core)
    relay = place(relay_of(me, 0))
    onward = place(far_of(source))

    barrier = pltpu.get_barrier_semaphore()
    for other in (sibling, place(source), place(relay_of(partner, 0))):
        pl.semaphore_signal(barrier, inc=1, device_id=other, device_id_type=MESH)
    operands = ((p_hbm, p_raw), (a_hbm, a_raw), (cols_hbm, cols), (agg_hbm, agg), (targ_hbm, targ))
    loads = [
        pltpu.make_async_copy(source, dest, load_sem.at[n])
        for n, (source, dest) in enumerate(operands)
    ]
    for load in loads:
        load.start()

    low = lax.broadcasted_iota(jnp.int32, (TILES, LANES), 1) < B
    low_block = lax.broadcasted_iota(jnp.int32, (B, LANES), 1) < B
    low_row = low[:8]

    loads[0].wait()
    for t in range(TILES):
        p_f32[pl.ds(t * ROWS, ROWS), :] = p_raw[:, pl.ds(t * LANES, LANES)].astype(F32)
    for j in range(ROWS // 2):
        one = p_f32[pl.ds(j, TILES, stride=ROWS), :]
        two = p_f32[pl.ds(j + 8, TILES, stride=ROWS), :]
        pair_f32[pl.ds(j * B, TILES, stride=2), :] = jnp.where(low, one, swap(two))
        pair_f32[pl.ds(j * B + 1, TILES, stride=2), :] = jnp.where(low, swap(one), two)
    for j in range(ROWS // 2):
        own_pairs[j] = pair_f32[pl.ds(j * B, B), :].astype(BF16)

    pl.semaphore_wait(barrier, 3)
    step = ROWS // 2 // CHUNKS
    chunks = [pl.ds(n * step, step) for n in range(CHUNKS)]
    to_relay = [
        pltpu.make_async_remote_copy(
            own_pairs.at[chunk],
            passing.at[chunk],
            send_sem.at[2 + n],
            recv_sem.at[2 + n],
            device_id=relay,
            device_id_type=MESH,
        )
        for n, chunk in enumerate(chunks)
    ]
    to_onward = [
        pltpu.make_async_remote_copy(
            passing.at[chunk],
            far_pairs.at[chunk],
            send_sem.at[2 + CHUNKS + n],
            recv_sem.at[2 + CHUNKS + n],
            device_id=onward,
            device_id_type=MESH,
        )
        for n, chunk in enumerate(chunks)
    ]
    to_sib = pltpu.make_async_remote_copy(
        own_pairs, sib_pairs, send_sem.at[1], recv_sem.at[1], device_id=sibling, device_id_type=MESH
    )
    for copy in to_relay:
        copy.start()
    to_sib.start()

    def pass_on():
        for n in range(CHUNKS):
            to_relay[n].wait_recv()
            to_onward[n].start()

    def unpack(source, left, right, start):
        def one(j, carry):
            both = source[j].astype(F32)
            turned = swap(both)
            left[start + j] = jnp.where(low_block, both, 0.0).astype(BF16)
            right[start + j] = jnp.where(low_block, 0.0, turned).astype(BF16)
            left[start + j + 8] = jnp.where(low_block, turned, 0.0).astype(BF16)
            right[start + j + 8] = jnp.where(low_block, 0.0, both).astype(BF16)
            return carry

        lax.fori_loop(0, ROWS // 2, one, 0)

    unpack(own_pairs, near_left, near_right, 0)
    pl.when(quick)(pass_on)
    for ref, end in (
        (near_left, 2 * ROWS),
        (near_right, 2 * ROWS),
        (far_left, ROWS),
        (far_right, ROWS),
    ):
        ref[end] = jnp.zeros((B, LANES), BF16)

    loads[1].wait()

    def widen(k, carry):
        for t in range(TILES):
            a_f32[pl.ds(k * TILES * ROWS + t * ROWS, ROWS), :] = a_raw[
                k, :, pl.ds(t * LANES, LANES)
            ].astype(F32)
        return carry

    lax.fori_loop(0, K, widen, 0)

    def arrange(i, carry):
        for n, (k, other) in enumerate(PAIRS):
            one = a_f32[pl.ds(k * TILES * ROWS + i, TILES, stride=ROWS), :]
            if other is None:
                even = jnp.where(low, one, 0.0)
                odd = jnp.where(low, swap(one), 0.0)
            else:
                two = a_f32[pl.ds(other * TILES * ROWS + i, TILES, stride=ROWS), :]
                even = jnp.where(low, one, swap(two))
                odd = jnp.where(low, swap(one), two)
            blocks[i * len(PAIRS) + n] = jnp.concatenate([even, odd], axis=0).astype(BF16)
        return carry

    lax.fori_loop(0, ROWS, arrange, 0)

    for load in loads[2:]:
        load.wait()
    first = me - core

    def transpose(pair, carry):
        halves = []
        for i in (2 * pair, 2 * pair + 1):
            x = p_f32[pl.ds(i, TILES, stride=ROWS), :]
            y = swap(x)
            keep = [jnp.where(agg[i] == first + c, 1.0, 0.0) for c in range(2)]
            halves.append(jnp.where(low, x * keep[0], y * keep[1]))
            halves.append(jnp.where(low, y * keep[0], x * keep[1]))
        pm_f32[...] = jnp.concatenate(halves, axis=0).T
        rows = [pm_f32[pl.ds(c * B + h, TILES, stride=2), :] for c in range(2) for h in range(2)]
        pm_t[pair] = jnp.concatenate(rows, axis=0).astype(BF16)
        return carry

    lax.fori_loop(0, ROWS // 2, transpose, 0)

    root = (me - 1) * ROWS

    def near_index(at):
        plane, at = at // ROWS, at % ROWS
        return jnp.where(plane == 1, at, jnp.where(plane == 2 - 2 * core, at + ROWS, 2 * ROWS))

    def far_index(at):
        plane, at = at // ROWS, at % ROWS
        return jnp.where(plane == 2 * core, at, ROWS)

    def multiply(pairs, left, right, index_of, initial):
        def group(g, carry):
            for r in range(GROUP):
                i = g * GROUP + r
                applied, slots = [], []
                for n, (k, other) in pairs:
                    above = left[index_of(cols[k, i] - root)]
                    slot = jnp.full((8, LANES), targ[k, i], jnp.int32)
                    if other is None:
                        below = jnp.zeros((B, LANES), BF16)
                    else:
                        below = right[index_of(cols[other, i] - root)]
                        slot = jnp.where(low_row, slot, targ[other, i])
                    applied.append(
                        jnp.dot(
                            blocks[i * len(PAIRS) + n],
                            jnp.concatenate([above, below], axis=0),
                            preferred_element_type=F32,
                        )
                    )
                    slots.append(slot)
                for s in range(KC):
                    summed = None
                    for value, slot in zip(applied, slots):
                        mask = jnp.concatenate([jnp.where(slot == s, 1.0, 0.0)] * 8, axis=0)
                        term = value * mask
                        summed = term if summed is None else summed + term
                    y_all[r, :, pl.ds(s * LANES, LANES)] = summed.astype(BF16)
            weights = jnp.concatenate(
                [pm_t[g * (GROUP // 2) + n] for n in range(GROUP // 2)], axis=1
            )
            partial = jnp.dot(
                weights,
                y_all[...].reshape(GROUP * B, KC * LANES),
                preferred_element_type=F32,
            )
            acc[...] += partial
            return carry

        if initial:
            acc[...] = jnp.zeros_like(acc)
        lax.fori_loop(0, ROWS // GROUP, group, 0)

    numbered = list(enumerate(PAIRS))
    to_sib.wait_recv()
    unpack(sib_pairs, near_left, near_right, ROWS)
    multiply(numbered, near_left, near_right, near_index, True)

    pl.when(jnp.logical_not(quick))(pass_on)
    for copy in to_onward:
        copy.wait_recv()
    unpack(far_pairs, far_left, far_right, 0)
    multiply(numbered[:3], far_left, far_right, far_index, False)

    def folded(c, s):
        even = acc[pl.ds(c * B, TILES), pl.ds(s * LANES, LANES)]
        odd = acc[pl.ds(c * B + TILES, TILES), pl.ds(s * LANES, LANES)]
        return jnp.where(low, even + swap(even), odd + swap(odd))

    for s in range(KC):
        part_out[s] = folded(1 - core, s)
    to_part = pltpu.make_async_remote_copy(
        part_out, part_in, send_sem.at[0], recv_sem.at[0], device_id=sibling, device_id_type=MESH
    )
    to_part.start()
    mine = [folded(core, s) for s in range(KC)]
    to_part.wait_recv()
    for s in range(KC):
        out[s] = mine[s] + part_in[s]
    for copy in (*to_relay, *to_onward, to_sib, to_part):
        copy.wait_send()


def local(n_wide, n_narrow, a_blocks, p_blocks, columns, aggregate, target):
    hbm = pl.BlockSpec(memory_space=pltpu.HBM)
    vmem = pltpu.VMEM
    smem = pltpu.SMEM
    operands = (columns.T, aggregate, target.T, p_blocks, jnp.transpose(a_blocks, (1, 0, 2)))
    result = pl.pallas_call(
        functools.partial(kernel, n_wide, n_narrow),
        out_shape=jax.ShapeDtypeStruct((KC, TILES, LANES), F32),
        in_specs=[hbm] * 5,
        out_specs=pl.BlockSpec(memory_space=pltpu.VMEM),
        scratch_shapes=[
            smem((K, ROWS), jnp.int32),
            smem((ROWS,), jnp.int32),
            smem((K, ROWS), jnp.int32),
            vmem((ROWS, B * B), BF16),
            vmem((K, ROWS, B * B), BF16),
            vmem((TILES * ROWS, LANES), F32),
            vmem((K * TILES * ROWS, LANES), F32),
            vmem((ROWS // 2 * B, LANES), F32),
            vmem((ROWS // 2, B, LANES), BF16),
            vmem((ROWS // 2, B, LANES), BF16),
            vmem((ROWS // 2, B, LANES), BF16),
            vmem((ROWS // 2, B, LANES), BF16),
            vmem((2 * ROWS + 1, B, LANES), BF16),
            vmem((2 * ROWS + 1, B, LANES), BF16),
            vmem((ROWS + 1, B, LANES), BF16),
            vmem((ROWS + 1, B, LANES), BF16),
            vmem((ROWS * len(PAIRS), B, LANES), BF16),
            vmem((GROUP, B, KC * LANES), BF16),
            vmem((LANES, LANES), F32),
            vmem((ROWS // 2, LANES, LANES), BF16),
            vmem((LANES, KC * LANES), F32),
            vmem((KC, TILES, LANES), F32),
            vmem((KC, TILES, LANES), F32),
            pltpu.SemaphoreType.DMA((5,)),
            pltpu.SemaphoreType.DMA((2 + 2 * CHUNKS,)),
            pltpu.SemaphoreType.DMA((2 + 2 * CHUNKS,)),
        ],
        compiler_params=pltpu.CompilerParams(
            collective_id=0, has_side_effects=True, vmem_limit_bytes=40 * 2**20
        ),
    )(*(pltpu.with_memory_space_constraint(value, pltpu.HBM) for value in operands))
    return result.reshape(1, KC, B * B)


def solution(mesh):
    placed = (
        P(("wide", "narrow"), None, None),
        P(("wide", "narrow"), None),
        P(("wide", "narrow"), None),
        P(("wide", "narrow")),
        P(("wide", "narrow"), None),
    )
    return jax.shard_map(
        functools.partial(local, mesh.shape["wide"], mesh.shape["narrow"]),
        mesh=mesh,
        in_specs=placed,
        out_specs=P(("wide", "narrow"), None, None),
        check_vma=False,
    )
```

time: 84.8 us -> 36.4 us (0.43)
  the two profiles are of different devices: /device:TPU:31 before, /device:TPU:7 now
where the time goes in v1:
time: 36.4 us; the launch traced here: 36.3 us
  Pallas kernels  35.6 us (98%)
  local copies, waits for them, and re-layouts  0.65 us (2%)
    pallas_call x1, Pallas kernels, local(): pl.pallas_call(functools.partial(kernel, n_wide, n_narrow), out_shape=jax...  35.6 us

profile of v1, /device:TPU:7, one launch (start us, length us, event | category | flops | bytes accessed | tf_op | source)
XLA Modules:
  0.0 36.3 jit_solution(5344202710920574878)
XLA Ops:
  0.0 35.6 %shard_map.55 = f32[7,32,128]{2,1,0:T(8,128)S(1)} custom-call(s32[7,16]{1,0:T(8,128)} %bitcast.6, s32[16]{0:T(128)} %agg_hbm.1, s32[7,16]{1,0:T(8,128)} %bitcast.7, bf16[16,4096]{1,0:T(8,128)(2,1)} %p_hbm.1, bf16[7,16,4096]{2,1,0:T(8,128)(2,1)} %bitcast.5), custom_call_target="tpu_custom_call" | custom-call | tf_op jit(solution)/shard_map/pallas_call | solution.py:308
  35.6 0.6 %copy.9 = f32[1,7,4096]{2,0,1:T(1,128)} copy(f32[1,7,4096]{2,0,1:T(1,128)S(1)} %bitcast.4) | data formatting | bytes 229376

commit v2 on v1

--- a/solution.py
+++ b/solution.py
@@ -113,6 +113,72 @@
     for j in range(ROWS // 2):
         own_pairs[j] = pair_f32[pl.ds(j * B, B), :].astype(BF16)
 
+    def unpack(source, left, right, start):
+        def one(j, carry):
+            both = source[j].astype(F32)
+            turned = swap(both)
+            left[start + j] = jnp.where(low_block, both, 0.0).astype(BF16)
+            right[start + j] = jnp.where(low_block, 0.0, turned).astype(BF16)
+            left[start + j + 8] = jnp.where(low_block, turned, 0.0).astype(BF16)
+            right[start + j + 8] = jnp.where(low_block, 0.0, both).astype(BF16)
+            return carry
+
+        lax.fori_loop(0, ROWS // 2, one, 0)
+
+    unpack(own_pairs, near_left, near_right, 0)
+    for ref, end in (
+        (near_left, 2 * ROWS),
+        (near_right, 2 * ROWS),
+        (far_left, ROWS),
+        (far_right, ROWS),
+    ):
+        ref[end] = jnp.zeros((B, LANES), BF16)
+
+    loads[1].wait()
+
+    def widen(k, carry):
+        for t in range(TILES):
+            a_f32[pl.ds(k * TILES * ROWS + t * ROWS, ROWS), :] = a_raw[
+                k, :, pl.ds(t * LANES, LANES)
+            ].astype(F32)
+        return carry
+
+    lax.fori_loop(0, K, widen, 0)
+
+    def arrange(i, carry):
+        for n, (k, other) in enumerate(PAIRS):
+            one = a_f32[pl.ds(k * TILES * ROWS + i, TILES, stride=ROWS), :]
+            if other is None:
+                even = jnp.where(low, one, 0.0)
+                odd = jnp.where(low, swap(one), 0.0)
+            else:
+                two = a_f32[pl.ds(other * TILES * ROWS + i, TILES, stride=ROWS), :]
+                even = jnp.where(low, one, swap(two))
+                odd = jnp.where(low, swap(one), two)
+            blocks[i * len(PAIRS) + n] = jnp.concatenate([even, odd], axis=0).astype(BF16)
+        return carry
+
+    lax.fori_loop(0, ROWS, arrange, 0)
+
+    for load in loads[2:]:
+        load.wait()
+    first = me - core
+
+    def transpose(pair, carry):
+        halves = []
+        for i in (2 * pair, 2 * pair + 1):
+            x = p_f32[pl.ds(i, TILES, stride=ROWS), :]
+            y = swap(x)
+            keep = [jnp.where(agg[i] == first + c, 1.0, 0.0) for c in range(2)]
+            halves.append(jnp.where(low, x * keep[0], y * keep[1]))
+            halves.append(jnp.where(low, y * keep[0], x * keep[1]))
+        pm_f32[...] = jnp.concatenate(halves, axis=0).T
+        rows = [pm_f32[pl.ds(c * B + h, TILES, stride=2), :] for c in range(2) for h in range(2)]
+        pm_t[pair] = jnp.concatenate(rows, axis=0).astype(BF16)
+        return carry
+
+    lax.fori_loop(0, ROWS // 2, transpose, 0)
+
     pl.semaphore_wait(barrier, 3)
     step = ROWS // 2 // CHUNKS
     chunks = [pl.ds(n * step, step) for n in range(CHUNKS)]
@@ -149,73 +215,6 @@
         for n in range(CHUNKS):
             to_relay[n].wait_recv()
             to_onward[n].start()
-
-    def unpack(source, left, right, start):
-        def one(j, carry):
-            both = source[j].astype(F32)
-            turned = swap(both)
-            left[start + j] = jnp.where(low_block, both, 0.0).astype(BF16)
-            right[start + j] = jnp.where(low_block, 0.0, turned).astype(BF16)
-            left[start + j + 8] = jnp.where(low_block, turned, 0.0).astype(BF16)
-            right[start + j + 8] = jnp.where(low_block, 0.0, both).astype(BF16)
-            return carry
-
-        lax.fori_loop(0, ROWS // 2, one, 0)
-
-    unpack(own_pairs, near_left, near_right, 0)
-    pl.when(quick)(pass_on)
-    for ref, end in (
-        (near_left, 2 * ROWS),
-        (near_right, 2 * ROWS),
-        (far_left, ROWS),
-        (far_right, ROWS),
-    ):
-        ref[end] = jnp.zeros((B, LANES), BF16)
-
-    loads[1].wait()
-
-    def widen(k, carry):
-        for t in range(TILES):
-            a_f32[pl.ds(k * TILES * ROWS + t * ROWS, ROWS), :] = a_raw[
-                k, :, pl.ds(t * LANES, LANES)
-            ].astype(F32)
-        return carry
-
-    lax.fori_loop(0, K, widen, 0)
-
-    def arrange(i, carry):
-        for n, (k, other) in enumerate(PAIRS):
-            one = a_f32[pl.ds(k * TILES * ROWS + i, TILES, stride=ROWS), :]
-            if other is None:
-                even = jnp.where(low, one, 0.0)
-                odd = jnp.where(low, swap(one), 0.0)
-            else:
-                two = a_f32[pl.ds(other * TILES * ROWS + i, TILES, stride=ROWS), :]
-                even = jnp.where(low, one, swap(two))
-                odd = jnp.where(low, swap(one), two)
-            blocks[i * len(PAIRS) + n] = jnp.concatenate([even, odd], axis=0).astype(BF16)
-        return carry
-
-    lax.fori_loop(0, ROWS, arrange, 0)
-
-    for load in loads[2:]:
-        load.wait()
-    first = me - core
-
-    def transpose(pair, carry):
-        halves = []
-        for i in (2 * pair, 2 * pair + 1):
-            x = p_f32[pl.ds(i, TILES, stride=ROWS), :]
-            y = swap(x)
-            keep = [jnp.where(agg[i] == first + c, 1.0, 0.0) for c in range(2)]
-            halves.append(jnp.where(low, x * keep[0], y * keep[1]))
-            halves.append(jnp.where(low, y * keep[0], x * keep[1]))
-        pm_f32[...] = jnp.concatenate(halves, axis=0).T
-        rows = [pm_f32[pl.ds(c * B + h, TILES, stride=2), :] for c in range(2) for h in range(2)]
-        pm_t[pair] = jnp.concatenate(rows, axis=0).astype(BF16)
-        return carry
-
-    lax.fori_loop(0, ROWS // 2, transpose, 0)
 
     root = (me - 1) * ROWS
 
@@ -273,6 +272,7 @@
     numbered = list(enumerate(PAIRS))
     to_sib.wait_recv()
     unpack(sib_pairs, near_left, near_right, ROWS)
+    pl.when(quick)(pass_on)
     multiply(numbered, near_left, near_right, near_index, True)
 
     pl.when(jnp.logical_not(quick))(pass_on)

time: 36.4 us -> 39 us (1.071)
  the two profiles are of different devices: /device:TPU:7 before, /device:TPU:39 now
where the time goes in v2:
time: 39 us; the launch traced here: 38.8 us
  Pallas kernels  38.2 us (98%)
  local copies, waits for them, and re-layouts  0.65 us (2%)
    pallas_call x1, Pallas kernels, local(): pl.pallas_call(functools.partial(kernel, n_wide, n_narrow), out_shape=jax...  38.2 us

profile of v2, /device:TPU:39, one launch (start us, length us, event | category | flops | bytes accessed | tf_op | source)
XLA Modules:
  0.0 38.8 jit_solution(7890175277690756639)
XLA Ops:
  0.0 38.2 %shard_map.55 = f32[7,32,128]{2,1,0:T(8,128)S(1)} custom-call(s32[7,16]{1,0:T(8,128)} %bitcast.6, s32[16]{0:T(128)} %agg_hbm.1, s32[7,16]{1,0:T(8,128)} %bitcast.7, bf16[16,4096]{1,0:T(8,128)(2,1)} %p_hbm.1, bf16[7,16,4096]{2,1,0:T(8,128)(2,1)} %bitcast.5), custom_call_target="tpu_custom_call" | custom-call | tf_op jit(solution)/shard_map/pallas_call | solution.py:308
  38.2 0.6 %copy.9 = f32[1,7,4096]{2,0,1:T(1,128)} copy(f32[1,7,4096]{2,0,1:T(1,128)S(1)} %bitcast.4) | data formatting | bytes 229376

commit v3 on v1

--- a/solution.py
+++ b/solution.py
@@ -13,6 +13,7 @@
 ROWS = 16
 TILES = 32
 LANES = 128
+HALF = 256
 PAIRS = ((1, 2), (3, 4), (5, 6), (0, None))
 GROUP = 4
 X_CHIPS = 4
@@ -41,8 +42,6 @@
     p_raw,
     a_raw,
     p_f32,
-    a_f32,
-    pair_f32,
     own_pairs,
     sib_pairs,
     passing,
@@ -53,8 +52,8 @@
     far_right,
     blocks,
     y_all,
-    pm_f32,
-    pm_t,
+    masked,
+    masked_t,
     acc,
     part_out,
     part_in,
@@ -98,20 +97,44 @@
     for load in loads:
         load.start()
 
-    low = lax.broadcasted_iota(jnp.int32, (TILES, LANES), 1) < B
-    low_block = lax.broadcasted_iota(jnp.int32, (B, LANES), 1) < B
+    def iota(rows, columns):
+        shape = (rows, columns)
+        return (lax.broadcasted_iota(jnp.int32, shape, 0), lax.broadcasted_iota(jnp.int32, shape, 1))
+
+    def ones_where(condition):
+        return jnp.where(condition, 1.0, 0.0).astype(BF16)
+
+    low = iota(ROWS, LANES)[1] < B
+    low_block = iota(B, LANES)[1] < B
+    low_tiles = iota(TILES, LANES)[1] < B
     low_row = low[:8]
 
+    row, column = iota(HALF, HALF)
+    turn = ones_where((row >> 4 == (column & 15)) & ((row & 15) == column >> 4))
+    row, column = iota(2 * HALF, HALF)
+    turn_twice = ones_where((row >> 5 == (column & 15)) & ((row >> 1 & 15) == column >> 4))
+
+    def stack(tile):
+        return jnp.concatenate([tile(t) for t in range(ROWS)], axis=0)
+
     loads[0].wait()
-    for t in range(TILES):
-        p_f32[pl.ds(t * ROWS, ROWS), :] = p_raw[:, pl.ds(t * LANES, LANES)].astype(F32)
+    flat = jnp.concatenate(
+        [
+            stack(lambda t, half=half: p_raw[:, pl.ds((half * ROWS + t) * LANES, LANES)])
+            for half in range(2)
+        ],
+        axis=1,
+    )
+    doubled = jnp.dot(turn_twice, flat, preferred_element_type=F32)
+    first_row = (iota(TILES, LANES)[0] & 1) == 0
     for j in range(ROWS // 2):
-        one = p_f32[pl.ds(j, TILES, stride=ROWS), :]
-        two = p_f32[pl.ds(j + 8, TILES, stride=ROWS), :]
-        pair_f32[pl.ds(j * B, TILES, stride=2), :] = jnp.where(low, one, swap(two))
-        pair_f32[pl.ds(j * B + 1, TILES, stride=2), :] = jnp.where(low, swap(one), two)
-    for j in range(ROWS // 2):
-        own_pairs[j] = pair_f32[pl.ds(j * B, B), :].astype(BF16)
+        for half in range(2):
+            lanes = slice(half * LANES, (half + 1) * LANES)
+            one = doubled[j * TILES : (j + 1) * TILES, lanes]
+            two = doubled[(j + 8) * TILES : (j + 9) * TILES, lanes]
+            left = jnp.where(first_row, one, swap(one))
+            right = jnp.where(first_row, swap(two), two)
+            own_pairs[j, pl.ds(half * TILES, TILES), :] = jnp.where(low_tiles, left, right).astype(BF16)
 
     pl.semaphore_wait(barrier, 3)
     step = ROWS // 2 // CHUNKS
@@ -150,6 +173,25 @@
             to_relay[n].wait_recv()
             to_onward[n].start()
 
+    loads[1].wait()
+    for n, (k, other) in enumerate(PAIRS):
+        for half in range(2):
+
+            def tile(t, which, half=half):
+                return a_raw[which, :, pl.ds((half * ROWS + t) * LANES, LANES)]
+
+            def side(h, t, k=k, other=other, tile=tile):
+                one = tile(t, k)[:, h * B : (h + 1) * B]
+                two = jnp.zeros_like(one) if other is None else tile(t, other)[:, h * B : (h + 1) * B]
+                return jnp.concatenate([one, two], axis=1)
+
+            both = jnp.concatenate(
+                [stack(functools.partial(side, h)) for h in range(2)], axis=1
+            )
+            turned = jnp.dot(turn, both, preferred_element_type=F32).astype(BF16)
+            for h in range(2):
+                blocks[n, 2 * h + half] = turned[:, h * LANES : (h + 1) * LANES]
+
     def unpack(source, left, right, start):
         def one(j, carry):
             both = source[j].astype(F32)
@@ -160,89 +202,73 @@
             right[start + j + 8] = jnp.where(low_block, 0.0, both).astype(BF16)
             return carry
 
-        lax.fori_loop(0, ROWS // 2, one, 0)
-
-    unpack(own_pairs, near_left, near_right, 0)
-    pl.when(quick)(pass_on)
-    for ref, end in (
-        (near_left, 2 * ROWS),
-        (near_right, 2 * ROWS),
-        (far_left, ROWS),
-        (far_right, ROWS),
-    ):
-        ref[end] = jnp.zeros((B, LANES), BF16)
-
-    loads[1].wait()
-
-    def widen(k, carry):
-        for t in range(TILES):
-            a_f32[pl.ds(k * TILES * ROWS + t * ROWS, ROWS), :] = a_raw[
-                k, :, pl.ds(t * LANES, LANES)
-            ].astype(F32)
-        return carry
-
-    lax.fori_loop(0, K, widen, 0)
-
-    def arrange(i, carry):
-        for n, (k, other) in enumerate(PAIRS):
-            one = a_f32[pl.ds(k * TILES * ROWS + i, TILES, stride=ROWS), :]
-            if other is None:
-                even = jnp.where(low, one, 0.0)
-                odd = jnp.where(low, swap(one), 0.0)
-            else:
-                two = a_f32[pl.ds(other * TILES * ROWS + i, TILES, stride=ROWS), :]
-                even = jnp.where(low, one, swap(two))
-                odd = jnp.where(low, swap(one), two)
-            blocks[i * len(PAIRS) + n] = jnp.concatenate([even, odd], axis=0).astype(BF16)
-        return carry
-
-    lax.fori_loop(0, ROWS, arrange, 0)
+        lax.fori_loop(0, ROWS // 2, one, 0, unroll=2)
+
+    def clear(left, right, start):
+        def one(j, carry):
+            left[start + j] = jnp.zeros((B, LANES), BF16)
+            right[start + j] = jnp.zeros((B, LANES), BF16)
+            return carry
+
+        lax.fori_loop(0, ROWS, one, 0, unroll=4)
+
+    far_start = 2 * ROWS * core
+    sib_start = 2 * ROWS - far_start
+    clear(near_left, near_right, far_start)
+    clear(far_left, far_right, ROWS)
+    clear(far_left, far_right, sib_start)
+    unpack(own_pairs, near_left, near_right, ROWS)
 
     for load in loads[2:]:
         load.wait()
     first = me - core
-
-    def transpose(pair, carry):
-        halves = []
-        for i in (2 * pair, 2 * pair + 1):
-            x = p_f32[pl.ds(i, TILES, stride=ROWS), :]
+    together = jnp.dot(turn, flat, preferred_element_type=F32)
+    p_f32[0] = together[:, :LANES]
+    p_f32[1] = together[:, LANES:]
+
+    def mask(i, carry):
+        keep = [jnp.where(agg[i] == first + c, 1.0, 0.0) for c in range(2)]
+        for half in range(2):
+            x = p_f32[half, pl.ds(pl.multiple_of(i * ROWS, ROWS), ROWS), :]
             y = swap(x)
-            keep = [jnp.where(agg[i] == first + c, 1.0, 0.0) for c in range(2)]
-            halves.append(jnp.where(low, x * keep[0], y * keep[1]))
-            halves.append(jnp.where(low, y * keep[0], x * keep[1]))
-        pm_f32[...] = jnp.concatenate(halves, axis=0).T
-        rows = [pm_f32[pl.ds(c * B + h, TILES, stride=2), :] for c in range(2) for h in range(2)]
-        pm_t[pair] = jnp.concatenate(rows, axis=0).astype(BF16)
+            masked[i, pl.ds(half * ROWS, ROWS), :] = jnp.where(low, x * keep[0], y * keep[1]).astype(BF16)
+            masked[i, pl.ds(TILES + half * ROWS, ROWS), :] = jnp.where(
+                low, y * keep[0], x * keep[1]
+            ).astype(BF16)
         return carry
 
-    lax.fori_loop(0, ROWS // 2, transpose, 0)
+    lax.fori_loop(0, ROWS, mask, 0, unroll=4)
+    row, column = iota(LANES, LANES)
+    order = ones_where(column == (row >> 6 << 6) + 2 * (row & 31) + (row >> 5 & 1))
+    masked_t[...] = lax.dot_general(
+        order,
+        masked[...].reshape(ROWS * B, LANES),
+        (((1,), (1,)), ((), ())),
+        preferred_element_type=F32,
+    ).astype(BF16)
 
     root = (me - 1) * ROWS
 
-    def near_index(at):
-        plane, at = at // ROWS, at % ROWS
-        return jnp.where(plane == 1, at, jnp.where(plane == 2 - 2 * core, at + ROWS, 2 * ROWS))
-
-    def far_index(at):
-        plane, at = at // ROWS, at % ROWS
-        return jnp.where(plane == 2 * core, at, ROWS)
-
-    def multiply(pairs, left, right, index_of, initial):
+    def entry(k, i):
+        return jnp.clip(cols[k, i] - root, 0, 3 * ROWS - 1)
+
+    def multiply(pairs, left, right):
         def group(g, carry):
             for r in range(GROUP):
                 i = g * GROUP + r
                 applied, slots = [], []
                 for n, (k, other) in pairs:
-                    above = left[index_of(cols[k, i] - root)]
+                    above = left[entry(k, i)]
                     slot = jnp.full((8, LANES), targ[k, i], jnp.int32)
                     if other is None:
                         below = jnp.zeros((B, LANES), BF16)
                     else:
-                        below = right[index_of(cols[other, i] - root)]
+                        below = right[entry(other, i)]
                         slot = jnp.where(low_row, slot, targ[other, i])
+                    rows = pl.ds(pl.multiple_of(i * ROWS, ROWS), ROWS)
                     applied.append(
                         jnp.dot(
-                            blocks[i * len(PAIRS) + n],
+                            jnp.concatenate([blocks[n, q, rows, :] for q in range(4)], axis=0),
                             jnp.concatenate([above, below], axis=0),
                             preferred_element_type=F32,
                         )
@@ -251,40 +277,35 @@
                 for s in range(KC):
                     summed = None
                     for value, slot in zip(applied, slots):
-                        mask = jnp.concatenate([jnp.where(slot == s, 1.0, 0.0)] * 8, axis=0)
-                        term = value * mask
+                        keep = jnp.concatenate([jnp.where(slot == s, 1.0, 0.0)] * 8, axis=0)
+                        term = value * keep
                         summed = term if summed is None else summed + term
-                    y_all[r, :, pl.ds(s * LANES, LANES)] = summed.astype(BF16)
-            weights = jnp.concatenate(
-                [pm_t[g * (GROUP // 2) + n] for n in range(GROUP // 2)], axis=1
-            )
-            partial = jnp.dot(
-                weights,
-                y_all[...].reshape(GROUP * B, KC * LANES),
-                preferred_element_type=F32,
-            )
-            acc[...] += partial
+                    y_all[i, :, pl.ds(s * LANES, LANES)] = summed.astype(BF16)
             return carry
 
-        if initial:
-            acc[...] = jnp.zeros_like(acc)
         lax.fori_loop(0, ROWS // GROUP, group, 0)
+        return jnp.dot(
+            masked_t[...],
+            y_all[...].reshape(ROWS * B, KC * LANES),
+            preferred_element_type=F32,
+        )
 
     numbered = list(enumerate(PAIRS))
     to_sib.wait_recv()
-    unpack(sib_pairs, near_left, near_right, ROWS)
-    multiply(numbered, near_left, near_right, near_index, True)
+    unpack(sib_pairs, near_left, near_right, sib_start)
+    pl.when(quick)(pass_on)
+    acc[...] = multiply(numbered, near_left, near_right)
 
     pl.when(jnp.logical_not(quick))(pass_on)
     for copy in to_onward:
         copy.wait_recv()
-    unpack(far_pairs, far_left, far_right, 0)
-    multiply(numbered[:3], far_left, far_right, far_index, False)
+    unpack(far_pairs, far_left, far_right, far_start)
+    acc[...] += multiply(numbered[:3], far_left, far_right)
 
     def folded(c, s):
         even = acc[pl.ds(c * B, TILES), pl.ds(s * LANES, LANES)]
         odd = acc[pl.ds(c * B + TILES, TILES), pl.ds(s * LANES, LANES)]
-        return jnp.where(low, even + swap(even), odd + swap(odd))
+        return jnp.where(low_tiles, even + swap(even), odd + swap(odd))
 
     for s in range(KC):
         part_out[s] = folded(1 - core, s)
@@ -316,21 +337,19 @@
             smem((K, ROWS), jnp.int32),
             vmem((ROWS, B * B), BF16),
             vmem((K, ROWS, B * B), BF16),
-            vmem((TILES * ROWS, LANES), F32),
-            vmem((K * TILES * ROWS, LANES), F32),
-            vmem((ROWS // 2 * B, LANES), F32),
+            vmem((2, HALF, LANES), F32),
             vmem((ROWS // 2, B, LANES), BF16),
             vmem((ROWS // 2, B, LANES), BF16),
             vmem((ROWS // 2, B, LANES), BF16),
             vmem((ROWS // 2, B, LANES), BF16),
-            vmem((2 * ROWS + 1, B, LANES), BF16),
-            vmem((2 * ROWS + 1, B, LANES), BF16),
-            vmem((ROWS + 1, B, LANES), BF16),
-            vmem((ROWS + 1, B, LANES), BF16),
-            vmem((ROWS * len(PAIRS), B, LANES), BF16),
-            vmem((GROUP, B, KC * LANES), BF16),
-            vmem((LANES, LANES), F32),
-            vmem((ROWS // 2, LANES, LANES), BF16),
+            vmem((3 * ROWS, B, LANES), BF16),
+            vmem((3 * ROWS, B, LANES), BF16),
+            vmem((3 * ROWS, B, LANES), BF16),
+            vmem((3 * ROWS, B, LANES), BF16),
+            vmem((len(PAIRS), 4, HALF, LANES), BF16),
+            vmem((ROWS, B, KC * LANES), BF16),
+            vmem((ROWS, B, LANES), BF16),
+            vmem((LANES, ROWS * B), BF16),
             vmem((LANES, KC * LANES), F32),
             vmem((KC, TILES, LANES), F32),
             vmem((KC, TILES, LANES), F32),

time: 36.4 us -> 35.7 us (0.981)
  Pallas kernels: 35.6 us -> 34.9 us
    pallas_call x1, Pallas kernels: 35.6 us -> 34.9 us  [local(): pl.pallas_call(functools.partial(kernel, n_wide, n_narrow), out_shape=jax...]
where the time goes in v3:
time: 35.7 us; the launch traced here: 35.5 us
  Pallas kernels  34.9 us (98%)
  local copies, waits for them, and re-layouts  0.65 us (2%)
    pallas_call x1, Pallas kernels, local(): pl.pallas_call(functools.partial(kernel, n_wide, n_narrow), out_shape=jax...  34.9 us

profile of v3, /device:TPU:7, one launch (start us, length us, event | category | flops | bytes accessed | tf_op | source)
XLA Modules:
  0.0 35.5 jit_solution(11796359332192799394)
XLA Ops:
  0.0 34.9 %shard_map.55 = f32[7,32,128]{2,1,0:T(8,128)S(1)} custom-call(s32[7,16]{1,0:T(8,128)} %bitcast.6, s32[16]{0:T(128)} %agg_hbm.1, s32[7,16]{1,0:T(8,128)} %bitcast.7, bf16[16,4096]{1,0:T(8,128)(2,1)} %p_hbm.1, bf16[7,16,4096]{2,1,0:T(8,128)(2,1)} %bitcast.5), custom_call_target="tpu_custom_call" | custom-call | tf_op jit(solution)/shard_map/pallas_call | solution.py:329
  34.9 0.6 %copy.9 = f32[1,7,4096]{2,0,1:T(1,128)} copy(f32[1,7,4096]{2,0,1:T(1,128)S(1)} %bitcast.4) | data formatting | bytes 229376

commit v4 on v3

--- a/solution.py
+++ b/solution.py
@@ -71,23 +71,23 @@
     def far_of(index):
         return (index - 1 + 2 * (index % 2) + total) % total
 
-    def relay_of(index, flipped):
+    def up(index, chips):
         wide, narrow = index // n_narrow, index % n_narrow
         z_lo, x = wide // X_CHIPS, wide % X_CHIPS
-        flip = (z_lo + index % 2 + flipped) % 2
         z_hi = narrow // 2 % 2
-        wide = (z_lo + 1 - 2 * (z_lo % 2)) * X_CHIPS + x
-        return wide * n_narrow + narrow + flip * (2 - 4 * z_hi)
-
+        z = (z_hi * z_run + z_lo + chips + 2 * z_run) % (2 * z_run)
+        return (z % z_run * X_CHIPS + x) * n_narrow + narrow + 2 * (z // z_run - z_hi)
+
+    z_run = n_wide // X_CHIPS
+    way = 1 - 2 * core
     partner = far_of(me)
-    source = relay_of(me, 1)
-    quick = (me // n_narrow // X_CHIPS + core) % 2 == 1
+    source = up(me, -way)
     sibling = place(me + 1 - 2 * core)
-    relay = place(relay_of(me, 0))
+    relay = place(up(me, way))
     onward = place(far_of(source))
 
     barrier = pltpu.get_barrier_semaphore()
-    for other in (sibling, place(source), place(relay_of(partner, 0))):
+    for other in (sibling, place(source), place(up(partner, -way))):
         pl.semaphore_signal(barrier, inc=1, device_id=other, device_id_type=MESH)
     operands = ((p_hbm, p_raw), (a_hbm, a_raw), (cols_hbm, cols), (agg_hbm, agg), (targ_hbm, targ))
     loads = [
@@ -126,16 +126,6 @@
         axis=1,
     )
     doubled = jnp.dot(turn_twice, flat, preferred_element_type=F32)
-    first_row = (iota(TILES, LANES)[0] & 1) == 0
-    for j in range(ROWS // 2):
-        for half in range(2):
-            lanes = slice(half * LANES, (half + 1) * LANES)
-            one = doubled[j * TILES : (j + 1) * TILES, lanes]
-            two = doubled[(j + 8) * TILES : (j + 9) * TILES, lanes]
-            left = jnp.where(first_row, one, swap(one))
-            right = jnp.where(first_row, swap(two), two)
-            own_pairs[j, pl.ds(half * TILES, TILES), :] = jnp.where(low_tiles, left, right).astype(BF16)
-
     pl.semaphore_wait(barrier, 3)
     step = ROWS // 2 // CHUNKS
     chunks = [pl.ds(n * step, step) for n in range(CHUNKS)]
@@ -164,14 +154,18 @@
     to_sib = pltpu.make_async_remote_copy(
         own_pairs, sib_pairs, send_sem.at[1], recv_sem.at[1], device_id=sibling, device_id_type=MESH
     )
-    for copy in to_relay:
-        copy.start()
+    first_row = (iota(TILES, LANES)[0] & 1) == 0
+    for j in range(ROWS // 2):
+        for half in range(2):
+            lanes = slice(half * LANES, (half + 1) * LANES)
+            one = doubled[j * TILES : (j + 1) * TILES, lanes]
+            two = doubled[(j + 8) * TILES : (j + 9) * TILES, lanes]
+            left = jnp.where(first_row, one, swap(one))
+            right = jnp.where(first_row, swap(two), two)
+            own_pairs[j, pl.ds(half * TILES, TILES), :] = jnp.where(low_tiles, left, right).astype(BF16)
+        if (j + 1) % step == 0:
+            to_relay[j // step].start()
     to_sib.start()
-
-    def pass_on():
-        for n in range(CHUNKS):
-            to_relay[n].wait_recv()
-            to_onward[n].start()
 
     loads[1].wait()
     for n, (k, other) in enumerate(PAIRS):
@@ -191,8 +185,10 @@
             turned = jnp.dot(turn, both, preferred_element_type=F32).astype(BF16)
             for h in range(2):
                 blocks[n, 2 * h + half] = turned[:, h * LANES : (h + 1) * LANES]
-
-    def unpack(source, left, right, start):
+        to_relay[n].wait_recv()
+        to_onward[n].start()
+
+    def unpack(source, left, right, start, begin=0, end=ROWS // 2):
         def one(j, carry):
             both = source[j].astype(F32)
             turned = swap(both)
@@ -202,7 +198,7 @@
             right[start + j + 8] = jnp.where(low_block, 0.0, both).astype(BF16)
             return carry
 
-        lax.fori_loop(0, ROWS // 2, one, 0, unroll=2)
+        lax.fori_loop(begin, end, one, 0, unroll=2)
 
     def clear(left, right, start):
         def one(j, carry):
@@ -293,13 +289,11 @@
     numbered = list(enumerate(PAIRS))
     to_sib.wait_recv()
     unpack(sib_pairs, near_left, near_right, sib_start)
-    pl.when(quick)(pass_on)
     acc[...] = multiply(numbered, near_left, near_right)
 
-    pl.when(jnp.logical_not(quick))(pass_on)
-    for copy in to_onward:
+    for n, copy in enumerate(to_onward):
         copy.wait_recv()
-    unpack(far_pairs, far_left, far_right, far_start)
+        unpack(far_pairs, far_left, far_right, far_start, n * step, (n + 1) * step)
     acc[...] += multiply(numbered[:3], far_left, far_right)
 
     def folded(c, s):

time: 35.7 us -> 37 us (1.036)
  the two profiles are of different devices: /device:TPU:7 before, /device:TPU:1 now
where the time goes in v4:
time: 37 us; the launch traced here: 36.9 us
  Pallas kernels  36.3 us (98%)
  local copies, waits for them, and re-layouts  0.65 us (2%)
    pallas_call x1, Pallas kernels, local(): pl.pallas_call(functools.partial(kernel, n_wide, n_narrow), out_shape=jax...  36.3 us

profile of v4, /device:TPU:1, one launch (start us, length us, event | category | flops | bytes accessed | tf_op | source)
XLA Modules:
  0.0 36.9 jit_solution(165305647795974826)
XLA Ops:
  0.0 36.3 %shard_map.55 = f32[7,32,128]{2,1,0:T(8,128)S(1)} custom-call(s32[7,16]{1,0:T(8,128)} %bitcast.6, s32[16]{0:T(128)} %agg_hbm.1, s32[7,16]{1,0:T(8,128)} %bitcast.7, bf16[16,4096]{1,0:T(8,128)(2,1)} %p_hbm.1, bf16[7,16,4096]{2,1,0:T(8,128)(2,1)} %bitcast.5), custom_call_target="tpu_custom_call" | custom-call | tf_op jit(solution)/shard_map/pallas_call | solution.py:323
  36.3 0.6 %copy.9 = f32[1,7,4096]{2,0,1:T(1,128)} copy(f32[1,7,4096]{2,0,1:T(1,128)S(1)} %bitcast.4) | data formatting | bytes 229376

commit v5 on v3

--- a/solution.py
+++ b/solution.py
@@ -17,7 +17,6 @@
 PAIRS = ((1, 2), (3, 4), (5, 6), (0, None))
 GROUP = 4
 X_CHIPS = 4
-CHUNKS = 4
 F32 = jnp.float32
 BF16 = jnp.bfloat16
 MESH = pl.DeviceIdType.MESH
@@ -44,7 +43,6 @@
     p_f32,
     own_pairs,
     sib_pairs,
-    passing,
     far_pairs,
     near_left,
     near_right,
@@ -71,23 +69,13 @@
     def far_of(index):
         return (index - 1 + 2 * (index % 2) + total) % total
 
-    def relay_of(index, flipped):
-        wide, narrow = index // n_narrow, index % n_narrow
-        z_lo, x = wide // X_CHIPS, wide % X_CHIPS
-        flip = (z_lo + index % 2 + flipped) % 2
-        z_hi = narrow // 2 % 2
-        wide = (z_lo + 1 - 2 * (z_lo % 2)) * X_CHIPS + x
-        return wide * n_narrow + narrow + flip * (2 - 4 * z_hi)
-
-    partner = far_of(me)
-    source = relay_of(me, 1)
-    quick = (me // n_narrow // X_CHIPS + core) % 2 == 1
+    first_wave = me // n_narrow // X_CHIPS < 4
+    at_once = jnp.logical_and(first_wave, me % n_narrow // 2 % 2 == 1)
     sibling = place(me + 1 - 2 * core)
-    relay = place(relay_of(me, 0))
-    onward = place(far_of(source))
+    distant = place(far_of(me))
 
     barrier = pltpu.get_barrier_semaphore()
-    for other in (sibling, place(source), place(relay_of(partner, 0))):
+    for other in (sibling, distant):
         pl.semaphore_signal(barrier, inc=1, device_id=other, device_id_type=MESH)
     operands = ((p_hbm, p_raw), (a_hbm, a_raw), (cols_hbm, cols), (agg_hbm, agg), (targ_hbm, targ))
     loads = [
@@ -136,42 +124,18 @@
             right = jnp.where(first_row, swap(two), two)
             own_pairs[j, pl.ds(half * TILES, TILES), :] = jnp.where(low_tiles, left, right).astype(BF16)
 
-    pl.semaphore_wait(barrier, 3)
-    step = ROWS // 2 // CHUNKS
-    chunks = [pl.ds(n * step, step) for n in range(CHUNKS)]
-    to_relay = [
-        pltpu.make_async_remote_copy(
-            own_pairs.at[chunk],
-            passing.at[chunk],
-            send_sem.at[2 + n],
-            recv_sem.at[2 + n],
-            device_id=relay,
-            device_id_type=MESH,
-        )
-        for n, chunk in enumerate(chunks)
-    ]
-    to_onward = [
-        pltpu.make_async_remote_copy(
-            passing.at[chunk],
-            far_pairs.at[chunk],
-            send_sem.at[2 + CHUNKS + n],
-            recv_sem.at[2 + CHUNKS + n],
-            device_id=onward,
-            device_id_type=MESH,
-        )
-        for n, chunk in enumerate(chunks)
-    ]
+    to_far = pltpu.make_async_remote_copy(
+        own_pairs, far_pairs, send_sem.at[0], recv_sem.at[0], device_id=distant, device_id_type=MESH
+    )
     to_sib = pltpu.make_async_remote_copy(
         own_pairs, sib_pairs, send_sem.at[1], recv_sem.at[1], device_id=sibling, device_id_type=MESH
     )
-    for copy in to_relay:
-        copy.start()
-    to_sib.start()
-
-    def pass_on():
-        for n in range(CHUNKS):
-            to_relay[n].wait_recv()
-            to_onward[n].start()
+
+    @pl.when(at_once)
+    def _():
+        pl.semaphore_wait(barrier, 2)
+        to_far.start()
+        to_sib.start()
 
     loads[1].wait()
     for n, (k, other) in enumerate(PAIRS):
@@ -291,14 +255,19 @@
         )
 
     numbered = list(enumerate(PAIRS))
+
+    @pl.when(jnp.logical_not(at_once))
+    def _():
+        pl.semaphore_wait(barrier, 2)
+        pl.when(first_wave)(to_far.start)
+        to_sib.start()
+
     to_sib.wait_recv()
     unpack(sib_pairs, near_left, near_right, sib_start)
-    pl.when(quick)(pass_on)
     acc[...] = multiply(numbered, near_left, near_right)
 
-    pl.when(jnp.logical_not(quick))(pass_on)
-    for copy in to_onward:
-        copy.wait_recv()
+    pl.when(jnp.logical_not(first_wave))(to_far.start)
+    to_far.wait_recv()
     unpack(far_pairs, far_left, far_right, far_start)
     acc[...] += multiply(numbered[:3], far_left, far_right)
 
@@ -310,14 +279,14 @@
     for s in range(KC):
         part_out[s] = folded(1 - core, s)
     to_part = pltpu.make_async_remote_copy(
-        part_out, part_in, send_sem.at[0], recv_sem.at[0], device_id=sibling, device_id_type=MESH
+        part_out, part_in, send_sem.at[2], recv_sem.at[2], device_id=sibling, device_id_type=MESH
     )
     to_part.start()
     mine = [folded(core, s) for s in range(KC)]
     to_part.wait_recv()
     for s in range(KC):
         out[s] = mine[s] + part_in[s]
-    for copy in (*to_relay, *to_onward, to_sib, to_part):
+    for copy in (to_far, to_sib, to_part):
         copy.wait_send()
 
 
@@ -341,7 +310,6 @@
             vmem((ROWS // 2, B, LANES), BF16),
             vmem((ROWS // 2, B, LANES), BF16),
             vmem((ROWS // 2, B, LANES), BF16),
-            vmem((ROWS // 2, B, LANES), BF16),
             vmem((3 * ROWS, B, LANES), BF16),
             vmem((3 * ROWS, B, LANES), BF16),
             vmem((3 * ROWS, B, LANES), BF16),
@@ -354,8 +322,8 @@
             vmem((KC, TILES, LANES), F32),
             vmem((KC, TILES, LANES), F32),
             pltpu.SemaphoreType.DMA((5,)),
-            pltpu.SemaphoreType.DMA((2 + 2 * CHUNKS,)),
-            pltpu.SemaphoreType.DMA((2 + 2 * CHUNKS,)),
+            pltpu.SemaphoreType.DMA((3,)),
+            pltpu.SemaphoreType.DMA((3,)),
         ],
         compiler_params=pltpu.CompilerParams(
             collective_id=0, has_side_effects=True, vmem_limit_bytes=40 * 2**20

time: 35.7 us -> 38.3 us (1.073)
  the two profiles are of different devices: /device:TPU:7 before, /device:TPU:161 now
where the time goes in v5:
time: 38.3 us; the launch traced here: 38.2 us
  Pallas kernels  37.5 us (98%)
  local copies, waits for them, and re-layouts  0.65 us (2%)
    pallas_call x1, Pallas kernels, local(): pl.pallas_call(functools.partial(kernel, n_wide, n_narrow), out_shape=jax...  37.5 us

profile of v5, /device:TPU:161, one launch (start us, length us, event | category | flops | bytes accessed | tf_op | source)
XLA Modules:
  0.0 38.2 jit_solution(567940612189255995)
XLA Ops:
  0.0 37.5 %shard_map.55 = f32[7,32,128]{2,1,0:T(8,128)S(1)} custom-call(s32[7,16]{1,0:T(8,128)} %bitcast.6, s32[16]{0:T(128)} %agg_hbm.1, s32[7,16]{1,0:T(8,128)} %bitcast.7, bf16[16,4096]{1,0:T(8,128)(2,1)} %p_hbm.1, bf16[7,16,4096]{2,1,0:T(8,128)(2,1)} %bitcast.5), custom_call_target="tpu_custom_call" | custom-call | tf_op jit(solution)/shard_map/pallas_call | solution.py:298
  37.5 0.6 %copy.9 = f32[1,7,4096]{2,0,1:T(1,128)} copy(f32[1,7,4096]{2,0,1:T(1,128)S(1)} %bitcast.4) | data formatting | bytes 229376

commit v6 on v5

--- a/solution.py
+++ b/solution.py
@@ -44,6 +44,7 @@
     own_pairs,
     sib_pairs,
     far_pairs,
+    passing,
     near_left,
     near_right,
     far_left,
@@ -69,14 +70,44 @@
     def far_of(index):
         return (index - 1 + 2 * (index % 2) + total) % total
 
-    first_wave = me // n_narrow // X_CHIPS < 4
-    at_once = jnp.logical_and(first_wave, me % n_narrow // 2 % 2 == 1)
+    wide, narrow = me // n_narrow, me % n_narrow
+    x, z_lo = wide % X_CHIPS, wide // X_CHIPS
+    z_run = n_wide // X_CHIPS
+    first_wave = jnp.logical_or(z_lo < 4, me == total - 1)
+    at_once = jnp.logical_and(first_wave, narrow // 2 % 2 == 1)
+
+    last_x, last = X_CHIPS - 1, n_narrow - 1
+
+    def both(*conditions):
+        return functools.reduce(jnp.logical_and, conditions)
+
+    def pick(condition, one, two):
+        return tuple(jnp.where(condition, a, b) for a, b in zip(one, two))
+
+    above = both(narrow == last, x == last_x, z_lo < z_run - 1)
+    below = both(narrow == 0, x == 0, z_lo > 0)
+    relayed = jnp.logical_or(above, below)
+    by_above = both(narrow == last - 2, x == last_x, z_lo > 0)
+    by_below = both(narrow == 2, x == 0, z_lo < z_run - 1)
+    passes = jnp.logical_or(by_above, by_below)
+    far = place(far_of(me))
+    down = ((z_lo + 1) * X_CHIPS + last_x, last - 2)
+    here = (z_lo * X_CHIPS + last_x, last - 2)
+    send_to = pick(above, down, pick(below, ((z_lo - 1) * X_CHIPS, 2), far))
+    come_from = pick(above, (z_lo * X_CHIPS, 2), pick(below, here, far))
+    pass_from = pick(by_above, ((z_lo - 1) * X_CHIPS + last_x, last), ((z_lo + 1) * X_CHIPS, 0))
+    pass_to = pick(by_above, (z_lo * X_CHIPS, 0), (z_lo * X_CHIPS + last_x, last))
     sibling = place(me + 1 - 2 * core)
-    distant = place(far_of(me))
 
     barrier = pltpu.get_barrier_semaphore()
-    for other in (sibling, distant):
+    for other in (sibling, come_from):
         pl.semaphore_signal(barrier, inc=1, device_id=other, device_id_type=MESH)
+
+    @pl.when(passes)
+    def _():
+        pl.semaphore_signal(barrier, inc=1, device_id=pass_from, device_id_type=MESH)
+
+    expected = jnp.where(passes, 3, 2)
     operands = ((p_hbm, p_raw), (a_hbm, a_raw), (cols_hbm, cols), (agg_hbm, agg), (targ_hbm, targ))
     loads = [
         pltpu.make_async_copy(source, dest, load_sem.at[n])
@@ -124,17 +155,26 @@
             right = jnp.where(first_row, swap(two), two)
             own_pairs[j, pl.ds(half * TILES, TILES), :] = jnp.where(low_tiles, left, right).astype(BF16)
 
-    to_far = pltpu.make_async_remote_copy(
-        own_pairs, far_pairs, send_sem.at[0], recv_sem.at[0], device_id=distant, device_id_type=MESH
+    def remote(source, dest, n, device):
+        return pltpu.make_async_remote_copy(
+            source, dest, send_sem.at[n], recv_sem.at[n], device_id=device, device_id_type=MESH
+        )
+
+    to_far = remote(own_pairs, far_pairs, 0, send_to)
+    to_sib = remote(own_pairs, sib_pairs, 1, sibling)
+    to_relay = remote(own_pairs, passing, 3, send_to)
+    to_pass = pltpu.make_async_remote_copy(
+        passing, far_pairs, send_sem.at[4], recv_sem.at[0], device_id=pass_to, device_id_type=MESH
     )
-    to_sib = pltpu.make_async_remote_copy(
-        own_pairs, sib_pairs, send_sem.at[1], recv_sem.at[1], device_id=sibling, device_id_type=MESH
-    )
+
+    def send_far():
+        pl.when(jnp.logical_not(relayed))(to_far.start)
+        pl.when(relayed)(to_relay.start)
 
     @pl.when(at_once)
     def _():
-        pl.semaphore_wait(barrier, 2)
-        to_far.start()
+        pl.semaphore_wait(barrier, expected)
+        send_far()
         to_sib.start()
 
     loads[1].wait()
@@ -258,15 +298,21 @@
 
     @pl.when(jnp.logical_not(at_once))
     def _():
-        pl.semaphore_wait(barrier, 2)
-        pl.when(first_wave)(to_far.start)
+        pl.semaphore_wait(barrier, expected)
+        pl.when(first_wave)(send_far)
         to_sib.start()
 
     to_sib.wait_recv()
     unpack(sib_pairs, near_left, near_right, sib_start)
     acc[...] = multiply(numbered, near_left, near_right)
 
-    pl.when(jnp.logical_not(first_wave))(to_far.start)
+    pl.when(jnp.logical_not(first_wave))(send_far)
+
+    @pl.when(passes)
+    def _():
+        to_relay.wait_recv()
+        to_pass.start()
+
     to_far.wait_recv()
     unpack(far_pairs, far_left, far_right, far_start)
     acc[...] += multiply(numbered[:3], far_left, far_right)
@@ -278,15 +324,16 @@
 
     for s in range(KC):
         part_out[s] = folded(1 - core, s)
-    to_part = pltpu.make_async_remote_copy(
-        part_out, part_in, send_sem.at[2], recv_sem.at[2], device_id=sibling, device_id_type=MESH
-    )
+    to_part = remote(part_out, part_in, 2, sibling)
     to_part.start()
     mine = [folded(core, s) for s in range(KC)]
     to_part.wait_recv()
     for s in range(KC):
         out[s] = mine[s] + part_in[s]
-    for copy in (to_far, to_sib, to_part):
+    pl.when(jnp.logical_not(relayed))(to_far.wait_send)
+    pl.when(relayed)(to_relay.wait_send)
+    pl.when(passes)(to_pass.wait_send)
+    for copy in (to_sib, to_part):
         copy.wait_send()
 
 
@@ -310,6 +357,7 @@
             vmem((ROWS // 2, B, LANES), BF16),
             vmem((ROWS // 2, B, LANES), BF16),
             vmem((ROWS // 2, B, LANES), BF16),
+            vmem((ROWS // 2, B, LANES), BF16),
             vmem((3 * ROWS, B, LANES), BF16),
             vmem((3 * ROWS, B, LANES), BF16),
             vmem((3 * ROWS, B, LANES), BF16),
@@ -322,8 +370,8 @@
             vmem((KC, TILES, LANES), F32),
             vmem((KC, TILES, LANES), F32),
             pltpu.SemaphoreType.DMA((5,)),
-            pltpu.SemaphoreType.DMA((3,)),
-            pltpu.SemaphoreType.DMA((3,)),
+            pltpu.SemaphoreType.DMA((5,)),
+            pltpu.SemaphoreType.DMA((5,)),
         ],
         compiler_params=pltpu.CompilerParams(
             collective_id=0, has_side_effects=True, vmem_limit_bytes=40 * 2**20

time: 38.3 us -> 41 us (1.070)
  Pallas kernels: 37.5 us -> 40.2 us
    pallas_call x1, Pallas kernels: 37.5 us -> 40.2 us  [local(): pl.pallas_call(functools.partial(kernel, n_wide, n_narrow), out_shape=jax...]
where the time goes in v6:
time: 41 us; the launch traced here: 40.9 us
  Pallas kernels  40.2 us (98%)
  local copies, waits for them, and re-layouts  0.65 us (2%)
    pallas_call x1, Pallas kernels, local(): pl.pallas_call(functools.partial(kernel, n_wide, n_narrow), out_shape=jax...  40.2 us

profile of v6, /device:TPU:161, one launch (start us, length us, event | category | flops | bytes accessed | tf_op | source)
XLA Modules:
  0.0 40.9 jit_solution(6597944754280628340)
XLA Ops:
  0.0 40.2 %shard_map.55 = f32[7,32,128]{2,1,0:T(8,128)S(1)} custom-call(s32[7,16]{1,0:T(8,128)} %bitcast.6, s32[16]{0:T(128)} %agg_hbm.1, s32[7,16]{1,0:T(8,128)} %bitcast.7, bf16[16,4096]{1,0:T(8,128)(2,1)} %p_hbm.1, bf16[7,16,4096]{2,1,0:T(8,128)(2,1)} %bitcast.5), custom_call_target="tpu_custom_call" | custom-call | tf_op jit(solution)/shard_map/pallas_call | solution.py:345
  40.2 0.6 %copy.9 = f32[1,7,4096]{2,0,1:T(1,128)} copy(f32[1,7,4096]{2,0,1:T(1,128)S(1)} %bitcast.4) | data formatting | bytes 229376

commit v7 on v5

--- a/solution.py
+++ b/solution.py
@@ -17,6 +17,7 @@
 PAIRS = ((1, 2), (3, 4), (5, 6), (0, None))
 GROUP = 4
 X_CHIPS = 4
+CHUNKS = 4
 F32 = jnp.float32
 BF16 = jnp.bfloat16
 MESH = pl.DeviceIdType.MESH
@@ -44,6 +45,7 @@
     own_pairs,
     sib_pairs,
     far_pairs,
+    passing,
     near_left,
     near_right,
     far_left,
@@ -69,13 +71,27 @@
     def far_of(index):
         return (index - 1 + 2 * (index % 2) + total) % total
 
-    first_wave = me // n_narrow // X_CHIPS < 4
+    def relay_of(index, flipped):
+        wide, narrow = index // n_narrow, index % n_narrow
+        z_lo, x = wide // X_CHIPS, wide % X_CHIPS
+        flip = (z_lo + index % 2 + flipped) % 2
+        z_hi = narrow // 2 % 2
+        wide = (z_lo + 1 - 2 * (z_lo % 2)) * X_CHIPS + x
+        return wide * n_narrow + narrow + flip * (2 - 4 * z_hi)
+
+    def in_first(index):
+        return jnp.logical_or(index // n_narrow // X_CHIPS < 4, index == total - 1)
+
+    source = relay_of(me, 1)
+    first_wave = in_first(me)
     at_once = jnp.logical_and(first_wave, me % n_narrow // 2 % 2 == 1)
+    quick = jnp.logical_and((me // n_narrow // X_CHIPS + core) % 2 == 1, in_first(source))
     sibling = place(me + 1 - 2 * core)
-    distant = place(far_of(me))
+    relay = place(relay_of(me, 0))
+    onward = place(far_of(source))
 
     barrier = pltpu.get_barrier_semaphore()
-    for other in (sibling, distant):
+    for other in (sibling, place(source), place(relay_of(far_of(me), 0))):
         pl.semaphore_signal(barrier, inc=1, device_id=other, device_id_type=MESH)
     operands = ((p_hbm, p_raw), (a_hbm, a_raw), (cols_hbm, cols), (agg_hbm, agg), (targ_hbm, targ))
     loads = [
@@ -124,17 +140,42 @@
             right = jnp.where(first_row, swap(two), two)
             own_pairs[j, pl.ds(half * TILES, TILES), :] = jnp.where(low_tiles, left, right).astype(BF16)
 
-    to_far = pltpu.make_async_remote_copy(
-        own_pairs, far_pairs, send_sem.at[0], recv_sem.at[0], device_id=distant, device_id_type=MESH
-    )
-    to_sib = pltpu.make_async_remote_copy(
-        own_pairs, sib_pairs, send_sem.at[1], recv_sem.at[1], device_id=sibling, device_id_type=MESH
-    )
+    def remote(source, dest, n, device):
+        return pltpu.make_async_remote_copy(
+            source, dest, send_sem.at[n], recv_sem.at[n], device_id=device, device_id_type=MESH
+        )
+
+    chunks = [pl.ds(n * 2, 2) for n in range(CHUNKS)]
+    to_sib = remote(own_pairs, sib_pairs, 0, sibling)
+    to_relay = [
+        remote(own_pairs.at[chunk], passing.at[chunk], 2 + n, relay) for n, chunk in enumerate(chunks)
+    ]
+    to_onward = [
+        remote(passing.at[chunk], far_pairs.at[chunk], 2 + CHUNKS + n, onward)
+        for n, chunk in enumerate(chunks)
+    ]
+
+    def send_far():
+        for copy in to_relay:
+            copy.start()
+
+    def pass_on(n):
+        to_relay[n].wait_recv()
+        to_onward[n].start()
+
+    def pass_all():
+        for n in range(CHUNKS):
+            pass_on(n)
+
+    pass_between = jnp.logical_and(at_once, quick)
+    pass_after = jnp.logical_and(jnp.logical_not(at_once), quick)
+    pass_half_way = jnp.logical_and(at_once, jnp.logical_not(quick))
+    pass_last = jnp.logical_not(jnp.logical_or(at_once, quick))
 
     @pl.when(at_once)
     def _():
-        pl.semaphore_wait(barrier, 2)
-        to_far.start()
+        pl.semaphore_wait(barrier, 3)
+        send_far()
         to_sib.start()
 
     loads[1].wait()
@@ -155,8 +196,9 @@
             turned = jnp.dot(turn, both, preferred_element_type=F32).astype(BF16)
             for h in range(2):
                 blocks[n, 2 * h + half] = turned[:, h * LANES : (h + 1) * LANES]
-
-    def unpack(source, left, right, start):
+        pl.when(pass_between)(functools.partial(pass_on, n))
+
+    def unpack(source, left, right, start, begin=0, end=ROWS // 2):
         def one(j, carry):
             both = source[j].astype(F32)
             turned = swap(both)
@@ -166,7 +208,7 @@
             right[start + j + 8] = jnp.where(low_block, 0.0, both).astype(BF16)
             return carry
 
-        lax.fori_loop(0, ROWS // 2, one, 0, unroll=2)
+        lax.fori_loop(begin, end, one, 0, unroll=2)
 
     def clear(left, right, start):
         def one(j, carry):
@@ -216,7 +258,7 @@
     def entry(k, i):
         return jnp.clip(cols[k, i] - root, 0, 3 * ROWS - 1)
 
-    def multiply(pairs, left, right):
+    def multiply(pairs, left, right, half_way):
         def group(g, carry):
             for r in range(GROUP):
                 i = g * GROUP + r
@@ -247,7 +289,9 @@
                     y_all[i, :, pl.ds(s * LANES, LANES)] = summed.astype(BF16)
             return carry
 
-        lax.fori_loop(0, ROWS // GROUP, group, 0)
+        lax.fori_loop(0, 2, group, 0)
+        half_way()
+        lax.fori_loop(2, 4, group, 0)
         return jnp.dot(
             masked_t[...],
             y_all[...].reshape(ROWS * B, KC * LANES),
@@ -258,18 +302,25 @@
 
     @pl.when(jnp.logical_not(at_once))
     def _():
-        pl.semaphore_wait(barrier, 2)
-        pl.when(first_wave)(to_far.start)
+        pl.semaphore_wait(barrier, 3)
+        pl.when(first_wave)(send_far)
         to_sib.start()
 
+    pl.when(pass_after)(pass_all)
     to_sib.wait_recv()
     unpack(sib_pairs, near_left, near_right, sib_start)
-    acc[...] = multiply(numbered, near_left, near_right)
-
-    pl.when(jnp.logical_not(first_wave))(to_far.start)
-    to_far.wait_recv()
-    unpack(far_pairs, far_left, far_right, far_start)
-    acc[...] += multiply(numbered[:3], far_left, far_right)
+
+    def half_way():
+        pl.when(jnp.logical_not(first_wave))(send_far)
+        pl.when(pass_half_way)(pass_all)
+
+    acc[...] = multiply(numbered, near_left, near_right, half_way)
+
+    pl.when(pass_last)(pass_all)
+    for n, copy in enumerate(to_onward):
+        copy.wait_recv()
+        unpack(far_pairs, far_left, far_right, far_start, 2 * n, 2 * n + 2)
+    acc[...] += multiply(numbered[:3], far_left, far_right, lambda: None)
 
     def folded(c, s):
         even = acc[pl.ds(c * B, TILES), pl.ds(s * LANES, LANES)]
@@ -278,15 +329,13 @@
 
     for s in range(KC):
         part_out[s] = folded(1 - core, s)
-    to_part = pltpu.make_async_remote_copy(
-        part_out, part_in, send_sem.at[2], recv_sem.at[2], device_id=sibling, device_id_type=MESH
-    )
+    to_part = remote(part_out, part_in, 1, sibling)
     to_part.start()
     mine = [folded(core, s) for s in range(KC)]
     to_part.wait_recv()
     for s in range(KC):
         out[s] = mine[s] + part_in[s]
-    for copy in (to_far, to_sib, to_part):
+    for copy in (*to_relay, *to_onward, to_sib, to_part):
         copy.wait_send()
 
 
@@ -310,6 +359,7 @@
             vmem((ROWS // 2, B, LANES), BF16),
             vmem((ROWS // 2, B, LANES), BF16),
             vmem((ROWS // 2, B, LANES), BF16),
+            vmem((ROWS // 2, B, LANES), BF16),
             vmem((3 * ROWS, B, LANES), BF16),
             vmem((3 * ROWS, B, LANES), BF16),
             vmem((3 * ROWS, B, LANES), BF16),
@@ -322,8 +372,8 @@
             vmem((KC, TILES, LANES), F32),
             vmem((KC, TILES, LANES), F32),
             pltpu.SemaphoreType.DMA((5,)),
-            pltpu.SemaphoreType.DMA((3,)),
-            pltpu.SemaphoreType.DMA((3,)),
+            pltpu.SemaphoreType.DMA((2 + 2 * CHUNKS,)),
+            pltpu.SemaphoreType.DMA((2 + 2 * CHUNKS,)),
         ],
         compiler_params=pltpu.CompilerParams(
             collective_id=0, has_side_effects=True, vmem_limit_bytes=40 * 2**20

time: 38.3 us -> 35.4 us (0.924)
  the two profiles are of different devices: /device:TPU:161 before, /device:TPU:1 now
where the time goes in v7:
time: 35.4 us; the launch traced here: 35.3 us
  Pallas kernels  34.6 us (98%)
  local copies, waits for them, and re-layouts  0.65 us (2%)
    pallas_call x1, Pallas kernels, local(): pl.pallas_call(functools.partial(kernel, n_wide, n_narrow), out_shape=jax...  34.6 us

profile of v7, /device:TPU:1, one launch (start us, length us, event | category | flops | bytes accessed | tf_op | source)
XLA Modules:
  0.0 35.3 jit_solution(9737316718010948206)
XLA Ops:
  0.0 34.6 %shard_map.55 = f32[7,32,128]{2,1,0:T(8,128)S(1)} custom-call(s32[7,16]{1,0:T(8,128)} %bitcast.6, s32[16]{0:T(128)} %agg_hbm.1, s32[7,16]{1,0:T(8,128)} %bitcast.7, bf16[16,4096]{1,0:T(8,128)(2,1)} %p_hbm.1, bf16[7,16,4096]{2,1,0:T(8,128)(2,1)} %bitcast.5), custom_call_target="tpu_custom_call" | custom-call | tf_op jit(solution)/shard_map/pallas_call | solution.py:347
  34.6 0.6 %copy.9 = f32[1,7,4096]{2,0,1:T(1,128)} copy(f32[1,7,4096]{2,0,1:T(1,128)S(1)} %bitcast.4) | data formatting | bytes 229376

commit v8 on v6

--- a/solution.py
+++ b/solution.py
@@ -73,41 +73,42 @@
     wide, narrow = me // n_narrow, me % n_narrow
     x, z_lo = wide % X_CHIPS, wide // X_CHIPS
     z_run = n_wide // X_CHIPS
+    last_x, last = X_CHIPS - 1, n_narrow - 1
+
+    def both(*conditions):
+        return functools.reduce(jnp.logical_and, conditions)
+
+    def pick(condition, one, two):
+        return tuple(jnp.where(condition, a, b) for a, b in zip(one, two))
+
     first_wave = jnp.logical_or(z_lo < 4, me == total - 1)
     at_once = jnp.logical_and(first_wave, narrow // 2 % 2 == 1)
 
-    last_x, last = X_CHIPS - 1, n_narrow - 1
-
-    def both(*conditions):
-        return functools.reduce(jnp.logical_and, conditions)
-
-    def pick(condition, one, two):
-        return tuple(jnp.where(condition, a, b) for a, b in zip(one, two))
-
-    above = both(narrow == last, x == last_x, z_lo < z_run - 1)
-    below = both(narrow == 0, x == 0, z_lo > 0)
+    odd = z_lo % 2 == 1
+    above = both(narrow == last, x == last_x, z_lo < z_run - 1, odd)
+    below = both(narrow == 0, x == 0, z_lo > 0, jnp.logical_not(odd))
     relayed = jnp.logical_or(above, below)
-    by_above = both(narrow == last - 2, x == last_x, z_lo > 0)
-    by_below = both(narrow == 2, x == 0, z_lo < z_run - 1)
+    by_above = both(narrow == last - 1, x == last_x, z_lo > 2, odd)
+    by_below = both(narrow == 1, x == 0, z_lo < z_run - 3, jnp.logical_not(odd))
     passes = jnp.logical_or(by_above, by_below)
     far = place(far_of(me))
-    down = ((z_lo + 1) * X_CHIPS + last_x, last - 2)
-    here = (z_lo * X_CHIPS + last_x, last - 2)
-    send_to = pick(above, down, pick(below, ((z_lo - 1) * X_CHIPS, 2), far))
-    come_from = pick(above, (z_lo * X_CHIPS, 2), pick(below, here, far))
-    pass_from = pick(by_above, ((z_lo - 1) * X_CHIPS + last_x, last), ((z_lo + 1) * X_CHIPS, 0))
-    pass_to = pick(by_above, (z_lo * X_CHIPS, 0), (z_lo * X_CHIPS + last_x, last))
+    on_above = ((z_lo + 2) * X_CHIPS + last_x, last - 1)
+    on_below = ((z_lo - 2) * X_CHIPS, 1)
+    send_to = pick(above, on_above, pick(below, on_below, far))
+    come_from = pick(above, ((z_lo - 1) * X_CHIPS, 1), pick(below, ((z_lo + 1) * X_CHIPS + last_x, last - 1), far))
+    pass_from = pick(by_above, ((z_lo - 2) * X_CHIPS + last_x, last), ((z_lo + 2) * X_CHIPS, 0))
+    pass_to = pick(by_above, ((z_lo - 1) * X_CHIPS, 0), ((z_lo + 1) * X_CHIPS + last_x, last))
     sibling = place(me + 1 - 2 * core)
 
     barrier = pltpu.get_barrier_semaphore()
-    for other in (sibling, come_from):
+
+    def greet(other):
         pl.semaphore_signal(barrier, inc=1, device_id=other, device_id_type=MESH)
 
-    @pl.when(passes)
-    def _():
-        pl.semaphore_signal(barrier, inc=1, device_id=pass_from, device_id_type=MESH)
-
-    expected = jnp.where(passes, 3, 2)
+    greet(sibling)
+    greet(come_from)
+    pl.when(passes)(functools.partial(greet, pass_from))
+    expected = 2 + jnp.where(passes, 1, 0)
     operands = ((p_hbm, p_raw), (a_hbm, a_raw), (cols_hbm, cols), (agg_hbm, agg), (targ_hbm, targ))
     loads = [
         pltpu.make_async_copy(source, dest, load_sem.at[n])

time: 41 us -> 36.9 us (0.90)
  Pallas kernels: 40.2 us -> 36.1 us
    pallas_call x1, Pallas kernels: 40.2 us -> 36.1 us  [local(): pl.pallas_call(functools.partial(kernel, n_wide, n_narrow), out_shape=jax...]
where the time goes in v8:
time: 36.9 us; the launch traced here: 36.8 us
  Pallas kernels  36.1 us (98%)
  local copies, waits for them, and re-layouts  0.65 us (2%)
    pallas_call x1, Pallas kernels, local(): pl.pallas_call(functools.partial(kernel, n_wide, n_narrow), out_shape=jax...  36.1 us

profile of v8, /device:TPU:161, one launch (start us, length us, event | category | flops | bytes accessed | tf_op | source)
XLA Modules:
  0.0 36.8 jit_solution(4644202258511967807)
XLA Ops:
  0.0 36.1 %shard_map.55 = f32[7,32,128]{2,1,0:T(8,128)S(1)} custom-call(s32[7,16]{1,0:T(8,128)} %bitcast.6, s32[16]{0:T(128)} %agg_hbm.1, s32[7,16]{1,0:T(8,128)} %bitcast.7, bf16[16,4096]{1,0:T(8,128)(2,1)} %p_hbm.1, bf16[7,16,4096]{2,1,0:T(8,128)(2,1)} %bitcast.5), custom_call_target="tpu_custom_call" | custom-call | tf_op jit(solution)/shard_map/pallas_call | solution.py:346
  36.2 0.6 %copy.9 = f32[1,7,4096]{2,0,1:T(1,128)} copy(f32[1,7,4096]{2,0,1:T(1,128)S(1)} %bitcast.4) | data formatting | bytes 229376

commit v9 on v8

--- a/solution.py
+++ b/solution.py
@@ -59,6 +59,7 @@
     load_sem,
     send_sem,
     recv_sem,
+    go_sem,
 ):
     total = n_wide * n_narrow
     me = lax.axis_index("wide") * n_narrow + lax.axis_index("narrow")
@@ -81,8 +82,15 @@
     def pick(condition, one, two):
         return tuple(jnp.where(condition, a, b) for a, b in zip(one, two))
 
-    first_wave = jnp.logical_or(z_lo < 4, me == total - 1)
+    quarter = z_run // 4
+    step = quarter * X_CHIPS * n_narrow
+    first_wave = jnp.logical_or(z_lo < 2 * quarter, me == total - 1)
     at_once = jnp.logical_and(first_wave, narrow // 2 % 2 == 1)
+    second_wave = jnp.logical_and(z_lo >= 2 * quarter, z_lo < 3 * quarter)
+    third_wave = jnp.logical_and(z_lo >= 3 * quarter, me != total - 1)
+    lets = jnp.logical_and(second_wave, me + step != total - 1)
+    held_up = place((me - step + total) % total)
+    let_go = place((me + step) % total)
 
     odd = z_lo % 2 == 1
     above = both(narrow == last, x == last_x, z_lo < z_run - 1, odd)
@@ -108,7 +116,8 @@
     greet(sibling)
     greet(come_from)
     pl.when(passes)(functools.partial(greet, pass_from))
-    expected = 2 + jnp.where(passes, 1, 0)
+    pl.when(third_wave)(functools.partial(greet, held_up))
+    expected = 2 + jnp.where(passes, 1, 0) + jnp.where(lets, 1, 0)
     operands = ((p_hbm, p_raw), (a_hbm, a_raw), (cols_hbm, cols), (agg_hbm, agg), (targ_hbm, targ))
     loads = [
         pltpu.make_async_copy(source, dest, load_sem.at[n])
@@ -257,7 +266,7 @@
     def entry(k, i):
         return jnp.clip(cols[k, i] - root, 0, 3 * ROWS - 1)
 
-    def multiply(pairs, left, right):
+    def multiply(pairs, left, right, half_way):
         def group(g, carry):
             for r in range(GROUP):
                 i = g * GROUP + r
@@ -288,7 +297,9 @@
                     y_all[i, :, pl.ds(s * LANES, LANES)] = summed.astype(BF16)
             return carry
 
-        lax.fori_loop(0, ROWS // GROUP, group, 0)
+        lax.fori_loop(0, 2, group, 0)
+        half_way()
+        lax.fori_loop(2, ROWS // GROUP, group, 0)
         return jnp.dot(
             masked_t[...],
             y_all[...].reshape(ROWS * B, KC * LANES),
@@ -305,18 +316,30 @@
 
     to_sib.wait_recv()
     unpack(sib_pairs, near_left, near_right, sib_start)
-    acc[...] = multiply(numbered, near_left, near_right)
-
-    pl.when(jnp.logical_not(first_wave))(send_far)
+    acc[...] = multiply(numbered, near_left, near_right, lambda: pl.when(second_wave)(send_far))
+
+    def far_sent():
+        pl.when(jnp.logical_not(relayed))(to_far.wait_send)
+        pl.when(relayed)(to_relay.wait_send)
+
+    @pl.when(lets)
+    def _():
+        far_sent()
+        pl.semaphore_signal(go_sem, inc=1, device_id=let_go, device_id_type=MESH)
 
     @pl.when(passes)
     def _():
         to_relay.wait_recv()
         to_pass.start()
 
+    @pl.when(third_wave)
+    def _():
+        pl.semaphore_wait(go_sem, 1)
+        send_far()
+
     to_far.wait_recv()
     unpack(far_pairs, far_left, far_right, far_start)
-    acc[...] += multiply(numbered[:3], far_left, far_right)
+    acc[...] += multiply(numbered[:3], far_left, far_right, lambda: None)
 
     def folded(c, s):
         even = acc[pl.ds(c * B, TILES), pl.ds(s * LANES, LANES)]
@@ -331,8 +354,7 @@
     to_part.wait_recv()
     for s in range(KC):
         out[s] = mine[s] + part_in[s]
-    pl.when(jnp.logical_not(relayed))(to_far.wait_send)
-    pl.when(relayed)(to_relay.wait_send)
+    pl.when(jnp.logical_not(lets))(far_sent)
     pl.when(passes)(to_pass.wait_send)
     for copy in (to_sib, to_part):
         copy.wait_send()
@@ -373,6 +395,7 @@
             pltpu.SemaphoreType.DMA((5,)),
             pltpu.SemaphoreType.DMA((5,)),
             pltpu.SemaphoreType.DMA((5,)),
+            pltpu.SemaphoreType.REGULAR,
         ],
         compiler_params=pltpu.CompilerParams(
             collective_id=0, has_side_effects=True, vmem_limit_bytes=40 * 2**20

time: 36.9 us -> 36.1 us (0.978)
  the two profiles are of different devices: /device:TPU:161 before, /device:TPU:225 now
where the time goes in v9:
time: 36.1 us; the launch traced here: 36 us
  Pallas kernels  35.4 us (98%)
  local copies, waits for them, and re-layouts  0.65 us (2%)
    pallas_call x1, Pallas kernels, local(): pl.pallas_call(functools.partial(kernel, n_wide, n_narrow), out_shape=jax...  35.4 us

profile of v9, /device:TPU:225, one launch (start us, length us, event | category | flops | bytes accessed | tf_op | source)
XLA Modules:
  0.0 36.0 jit_solution(2686418724220650420)
XLA Ops:
  0.0 35.4 %shard_map.55 = f32[7,32,128]{2,1,0:T(8,128)S(1)} custom-call(s32[7,16]{1,0:T(8,128)} %bitcast.6, s32[16]{0:T(128)} %agg_hbm.1, s32[7,16]{1,0:T(8,128)} %bitcast.7, bf16[16,4096]{1,0:T(8,128)(2,1)} %p_hbm.1, bf16[7,16,4096]{2,1,0:T(8,128)(2,1)} %bitcast.5), custom_call_target="tpu_custom_call" | custom-call | tf_op jit(solution)/shard_map/pallas_call | solution.py:368
  35.4 0.6 %copy.9 = f32[1,7,4096]{2,0,1:T(1,128)} copy(f32[1,7,4096]{2,0,1:T(1,128)S(1)} %bitcast.4) | data formatting | bytes 229376

commit v10 on v8

--- a/solution.py
+++ b/solution.py
@@ -81,8 +81,11 @@
     def pick(condition, one, two):
         return tuple(jnp.where(condition, a, b) for a, b in zip(one, two))
 
-    first_wave = jnp.logical_or(z_lo < 4, me == total - 1)
+    quarter = z_run // 4
+    first_wave = jnp.logical_or(z_lo < 2 * quarter, me == total - 1)
     at_once = jnp.logical_and(first_wave, narrow // 2 % 2 == 1)
+    second_wave = jnp.logical_and(z_lo >= 2 * quarter, z_lo < 3 * quarter)
+    third_wave = jnp.logical_and(z_lo >= 3 * quarter, me != total - 1)
 
     odd = z_lo % 2 == 1
     above = both(narrow == last, x == last_x, z_lo < z_run - 1, odd)
@@ -257,7 +260,7 @@
     def entry(k, i):
         return jnp.clip(cols[k, i] - root, 0, 3 * ROWS - 1)
 
-    def multiply(pairs, left, right):
+    def multiply(pairs, left, right, half_way):
         def group(g, carry):
             for r in range(GROUP):
                 i = g * GROUP + r
@@ -288,7 +291,9 @@
                     y_all[i, :, pl.ds(s * LANES, LANES)] = summed.astype(BF16)
             return carry
 
-        lax.fori_loop(0, ROWS // GROUP, group, 0)
+        lax.fori_loop(0, 2, group, 0)
+        half_way()
+        lax.fori_loop(2, ROWS // GROUP, group, 0)
         return jnp.dot(
             masked_t[...],
             y_all[...].reshape(ROWS * B, KC * LANES),
@@ -305,9 +310,9 @@
 
     to_sib.wait_recv()
     unpack(sib_pairs, near_left, near_right, sib_start)
-    acc[...] = multiply(numbered, near_left, near_right)
-
-    pl.when(jnp.logical_not(first_wave))(send_far)
+    acc[...] = multiply(numbered, near_left, near_right, lambda: pl.when(second_wave)(send_far))
+
+    pl.when(third_wave)(send_far)
 
     @pl.when(passes)
     def _():
@@ -316,7 +321,7 @@
 
     to_far.wait_recv()
     unpack(far_pairs, far_left, far_right, far_start)
-    acc[...] += multiply(numbered[:3], far_left, far_right)
+    acc[...] += multiply(numbered[:3], far_left, far_right, lambda: None)
 
     def folded(c, s):
         even = acc[pl.ds(c * B, TILES), pl.ds(s * LANES, LANES)]

time: 36.9 us -> 36 us (0.976)
  the two profiles are of different devices: /device:TPU:161 before, /device:TPU:193 now
where the time goes in v10:
time: 36 us; the launch traced here: 35.9 us
  Pallas kernels  35.2 us (98%)
  local copies, waits for them, and re-layouts  0.65 us (2%)
    pallas_call x1, Pallas kernels, local(): pl.pallas_call(functools.partial(kernel, n_wide, n_narrow), out_shape=jax...  35.2 us

profile of v10, /device:TPU:193, one launch (start us, length us, event | category | flops | bytes accessed | tf_op | source)
XLA Modules:
  0.0 35.9 jit_solution(13248993174071876356)
XLA Ops:
  0.0 35.2 %shard_map.55 = f32[7,32,128]{2,1,0:T(8,128)S(1)} custom-call(s32[7,16]{1,0:T(8,128)} %bitcast.6, s32[16]{0:T(128)} %agg_hbm.1, s32[7,16]{1,0:T(8,128)} %bitcast.7, bf16[16,4096]{1,0:T(8,128)(2,1)} %p_hbm.1, bf16[7,16,4096]{2,1,0:T(8,128)(2,1)} %bitcast.5), custom_call_target="tpu_custom_call" | custom-call | tf_op jit(solution)/shard_map/pallas_call | solution.py:351
  35.2 0.6 %copy.9 = f32[1,7,4096]{2,0,1:T(1,128)} copy(f32[1,7,4096]{2,0,1:T(1,128)S(1)} %bitcast.4) | data formatting | bytes 229376

commit v11 on v10

--- a/solution.py
+++ b/solution.py
@@ -82,17 +82,16 @@
         return tuple(jnp.where(condition, a, b) for a, b in zip(one, two))
 
     quarter = z_run // 4
-    first_wave = jnp.logical_or(z_lo < 2 * quarter, me == total - 1)
-    at_once = jnp.logical_and(first_wave, narrow // 2 % 2 == 1)
-    second_wave = jnp.logical_and(z_lo >= 2 * quarter, z_lo < 3 * quarter)
-    third_wave = jnp.logical_and(z_lo >= 3 * quarter, me != total - 1)
-
     odd = z_lo % 2 == 1
     above = both(narrow == last, x == last_x, z_lo < z_run - 1, odd)
     below = both(narrow == 0, x == 0, z_lo > 0, jnp.logical_not(odd))
     relayed = jnp.logical_or(above, below)
     by_above = both(narrow == last - 1, x == last_x, z_lo > 2, odd)
     by_below = both(narrow == 1, x == 0, z_lo < z_run - 3, jnp.logical_not(odd))
+    first_wave = jnp.logical_or(relayed, jnp.logical_or(z_lo < 2 * quarter, me == total - 1))
+    at_once = jnp.logical_and(first_wave, narrow // 2 % 2 == 1)
+    second_wave = jnp.logical_and(jnp.logical_not(first_wave), z_lo < 3 * quarter)
+    third_wave = jnp.logical_and(jnp.logical_not(first_wave), z_lo >= 3 * quarter)
     passes = jnp.logical_or(by_above, by_below)
     far = place(far_of(me))
     on_above = ((z_lo + 2) * X_CHIPS + last_x, last - 1)
@@ -310,14 +309,17 @@
 
     to_sib.wait_recv()
     unpack(sib_pairs, near_left, near_right, sib_start)
-    acc[...] = multiply(numbered, near_left, near_right, lambda: pl.when(second_wave)(send_far))
+    def half_way():
+        pl.when(second_wave)(send_far)
+
+        @pl.when(passes)
+        def _():
+            to_relay.wait_recv()
+            to_pass.start()
+
+    acc[...] = multiply(numbered, near_left, near_right, half_way)
 
     pl.when(third_wave)(send_far)
-
-    @pl.when(passes)
-    def _():
-        to_relay.wait_recv()
-        to_pass.start()
 
     to_far.wait_recv()
     unpack(far_pairs, far_left, far_right, far_start)

time: 36 us -> 35.2 us (0.978)
  the two profiles are of different devices: /device:TPU:193 before, /device:TPU:225 now
where the time goes in v11:
time: 35.2 us; the launch traced here: 35.1 us
  Pallas kernels  34.4 us (98%)
  local copies, waits for them, and re-layouts  0.65 us (2%)
    pallas_call x1, Pallas kernels, local(): pl.pallas_call(functools.partial(kernel, n_wide, n_narrow), out_shape=jax...  34.4 us

profile of v11, /device:TPU:225, one launch (start us, length us, event | category | flops | bytes accessed | tf_op | source)
XLA Modules:
  0.0 35.1 jit_solution(12885857420307486955)
XLA Ops:
  0.0 34.4 %shard_map.55 = f32[7,32,128]{2,1,0:T(8,128)S(1)} custom-call(s32[7,16]{1,0:T(8,128)} %bitcast.6, s32[16]{0:T(128)} %agg_hbm.1, s32[7,16]{1,0:T(8,128)} %bitcast.7, bf16[16,4096]{1,0:T(8,128)(2,1)} %p_hbm.1, bf16[7,16,4096]{2,1,0:T(8,128)(2,1)} %bitcast.5), custom_call_target="tpu_custom_call" | custom-call | tf_op jit(solution)/shard_map/pallas_call | solution.py:353
  34.4 0.6 %copy.9 = f32[1,7,4096]{2,0,1:T(1,128)} copy(f32[1,7,4096]{2,0,1:T(1,128)S(1)} %bitcast.4) | data formatting | bytes 229376

commit v12 on v11

--- a/solution.py
+++ b/solution.py
@@ -309,8 +309,9 @@
 
     to_sib.wait_recv()
     unpack(sib_pairs, near_left, near_right, sib_start)
+    pl.when(second_wave)(send_far)
     def half_way():
-        pl.when(second_wave)(send_far)
+        pl.when(third_wave)(send_far)
 
         @pl.when(passes)
         def _():
@@ -318,8 +319,6 @@
             to_pass.start()
 
     acc[...] = multiply(numbered, near_left, near_right, half_way)
-
-    pl.when(third_wave)(send_far)
 
     to_far.wait_recv()
     unpack(far_pairs, far_left, far_right, far_start)

time: 35.2 us -> 34.6 us (0.983)
  the two profiles are of different devices: /device:TPU:225 before, /device:TPU:33 now
where the time goes in v12:
time: 34.6 us; the launch traced here: 34.4 us
  Pallas kernels  33.8 us (98%)
  local copies, waits for them, and re-layouts  0.65 us (2%)
    pallas_call x1, Pallas kernels, local(): pl.pallas_call(functools.partial(kernel, n_wide, n_narrow), out_shape=jax...  33.8 us

profile of v12, /device:TPU:33, one launch (start us, length us, event | category | flops | bytes accessed | tf_op | source)
XLA Modules:
  0.0 34.4 jit_solution(16133045499700035118)
XLA Ops:
  0.0 33.8 %shard_map.55 = f32[7,32,128]{2,1,0:T(8,128)S(1)} custom-call(s32[7,16]{1,0:T(8,128)} %bitcast.6, s32[16]{0:T(128)} %agg_hbm.1, s32[7,16]{1,0:T(8,128)} %bitcast.7, bf16[16,4096]{1,0:T(8,128)(2,1)} %p_hbm.1, bf16[7,16,4096]{2,1,0:T(8,128)(2,1)} %bitcast.5), custom_call_target="tpu_custom_call" | custom-call | tf_op jit(solution)/shard_map/pallas_call | solution.py:352
  33.8 0.6 %copy.9 = f32[1,7,4096]{2,0,1:T(1,128)} copy(f32[1,7,4096]{2,0,1:T(1,128)S(1)} %bitcast.4) | data formatting | bytes 229376

commit v13 on v12

--- a/solution.py
+++ b/solution.py
@@ -88,7 +88,7 @@
     relayed = jnp.logical_or(above, below)
     by_above = both(narrow == last - 1, x == last_x, z_lo > 2, odd)
     by_below = both(narrow == 1, x == 0, z_lo < z_run - 3, jnp.logical_not(odd))
-    first_wave = jnp.logical_or(relayed, jnp.logical_or(z_lo < 2 * quarter, me == total - 1))
+    first_wave = jnp.logical_or(relayed, jnp.logical_or(z_lo < 2 * quarter - 1, me == total - 1))
     at_once = jnp.logical_and(first_wave, narrow // 2 % 2 == 1)
     second_wave = jnp.logical_and(jnp.logical_not(first_wave), z_lo < 3 * quarter)
     third_wave = jnp.logical_and(jnp.logical_not(first_wave), z_lo >= 3 * quarter)

time: 34.6 us -> 35.8 us (1.035)
  the two profiles are of different devices: /device:TPU:33 before, /device:TPU:103 now
where the time goes in v13:
time: 35.8 us; the launch traced here: 35.6 us
  Pallas kernels  35 us (98%)
  local copies, waits for them, and re-layouts  0.65 us (2%)
    pallas_call x1, Pallas kernels, local(): pl.pallas_call(functools.partial(kernel, n_wide, n_narrow), out_shape=jax...  35 us

profile of v13, /device:TPU:103, one launch (start us, length us, event | category | flops | bytes accessed | tf_op | source)
XLA Modules:
  0.0 35.6 jit_solution(3749947174301475847)
XLA Ops:
  0.0 35.0 %shard_map.55 = f32[7,32,128]{2,1,0:T(8,128)S(1)} custom-call(s32[7,16]{1,0:T(8,128)} %bitcast.6, s32[16]{0:T(128)} %agg_hbm.1, s32[7,16]{1,0:T(8,128)} %bitcast.7, bf16[16,4096]{1,0:T(8,128)(2,1)} %p_hbm.1, bf16[7,16,4096]{2,1,0:T(8,128)(2,1)} %bitcast.5), custom_call_target="tpu_custom_call" | custom-call | tf_op jit(solution)/shard_map/pallas_call | solution.py:352
  35.0 0.6 %copy.9 = f32[1,7,4096]{2,0,1:T(1,128)} copy(f32[1,7,4096]{2,0,1:T(1,128)S(1)} %bitcast.4) | data formatting | bytes 229376
